TPU v7x, 32 devices: a whole 2x2x4 slice. The times are simulated.
32 devices in a mesh: dp: 8 (over y, x, core), tensor: 4 (over z).
Axes of the slice: x: 2, y: 2, z: 4, core: 2. Of those that a mesh axis runs over, the one named last changes fastest.
Arguments:
- images: bfloat16 [24, 196, 768], P('dp'), may hold values from -6 to 6
- cotangent: bfloat16 [24, 196, 768], P('dp'), may hold values from -6 to 6
- norm_gains: bfloat16 [2, 768], P(None, 'dp'), may hold values from 0.099609375 to 1.8984375
- norm_shifts: bfloat16 [2, 768], P(None, 'dp'), may hold values from -1.5 to 1.5
- tok_in: bfloat16 [196, 384], P(None, 'dp'), may hold values from -0.4375 to 0.4375
- tok_out_t: bfloat16 [196, 384], P(None, 'dp'), may hold values from -0.3125 to 0.3125
- tok_bias_in: bfloat16 [1, 384], P(None, 'dp'), may hold values from -1.5 to 1.5
- tok_bias_out: bfloat16 [196], replicated, may hold values from -1.5 to 1.5
- w_in: bfloat16 [768, 3072], P(None, 'tensor'), may hold values from -0.21875 to 0.21875
- bias_in: bfloat16 [3072], P('tensor'), may hold values from -1.5 to 1.5
- w_out: bfloat16 [3072, 768], P('tensor'), may hold values from -0.109375 to 0.109375
- bias_out: bfloat16 [768], replicated, may hold values from -1.5 to 1.5
Outputs:
- activations: bfloat16 [24, 196, 768], P('dp')
- input_grad: bfloat16 [24, 196, 768], P('dp')
- grad_norm_gains: float32 [2, 768], P(None, 'dp')
- grad_norm_shifts: float32 [2, 768], P(None, 'dp')
- grad_tok_in: float32 [196, 384], P(None, 'dp')
- grad_tok_out_t: float32 [196, 384], P(None, 'dp')
- grad_tok_bias_in: float32 [1, 384], P(None, 'dp')
- grad_tok_bias_out: float32 [196], replicated
- grad_w_in: float32 [768, 3072], P('dp', 'tensor')
- grad_bias_in: float32 [3072], P(('tensor', 'dp'))
- grad_w_out: float32 [3072, 768], P('tensor', 'dp')
- grad_bias_out: float32 [768], P('dp')
- sqnorms: float32 [24], P('dp')
- influence: float32 [8, 16], P(None, 'dp')
All inputs are finite; a program needn't handle non-finite values.
Results may differ from a plain program's by a relative error of at most 0.0073.
Values may be sent and summed in bfloat16 or wider, within the bound.
A program may use at most 512 MiB of HBM per device.

v0:
```python
import jax
import jax.numpy as jnp
from jax import lax
from jax.sharding import PartitionSpec as P

D = 768
FF = 3072
QRY_DEV = 1


HIGH = lax.Precision.HIGHEST


def layer_norm(values, gain, shift):
    center = values - jnp.mean(values, axis=-1, keepdims=True)
    spread = jnp.mean(center * center, axis=-1, keepdims=True)
    return center * lax.rsqrt(spread + 1e-06) * gain + shift


def smooth(values):
    return jax.nn.gelu(values, approximate=True)


def contract(left, right, left_dim, right_dim):
    return lax.dot_general(
        left, right, (((left_dim,), (right_dim,)), ((), ())), preferred_element_type=jnp.float32
    )


def per_device(
    images,
    cotangent,
    norm_gains,
    norm_shifts,
    tok_in,
    tok_out_t,
    tok_bias_in,
    tok_bias_out,
    w_in,
    bias_in,
    w_out,
    bias_out,
):
    gains, shifts, tok_first, tok_second, tok_bias = (
        lax.all_gather(norm_gains, "dp", axis=1, tiled=True),
        lax.all_gather(norm_shifts, "dp", axis=1, tiled=True),
        lax.all_gather(tok_in, "dp", axis=1, tiled=True),
        lax.all_gather(tok_out_t, "dp", axis=1, tiled=True),
        lax.all_gather(tok_bias_in, "dp", axis=1, tiled=True),
    )
    gains = gains.astype(jnp.float32)
    shifts = shifts.astype(jnp.float32)
    count, patches, width = images.shape
    rows = count * patches
    inputs = images.astype(jnp.float32)
    normed_one, first_back = jax.vjp(layer_norm, inputs, gains[0], shifts[0])
    normed_low = normed_one.astype(jnp.bfloat16)
    tok_pre = (
        jnp.einsum("sk,nsd->nkd", tok_first, normed_low, preferred_element_type=jnp.float32)
        + tok_bias[0].astype(jnp.float32)[None, :, None]
    )
    tok_hidden = smooth(tok_pre).astype(jnp.bfloat16)
    tok_mixed = (
        jnp.einsum("sk,nkd->nsd", tok_second, tok_hidden, preferred_element_type=jnp.float32)
        + tok_bias_out.astype(jnp.float32)[None, :, None]
    )
    resid = inputs + tok_mixed
    normed_two, second_back = jax.vjp(layer_norm, resid, gains[1], shifts[1])
    chan_in = normed_two.astype(jnp.bfloat16).reshape(rows, width)
    chan_pre = jnp.dot(chan_in, w_in, preferred_element_type=jnp.float32) + bias_in.astype(
        jnp.float32
    )
    hidden = smooth(chan_pre).astype(jnp.bfloat16)
    partial_out = jnp.dot(hidden, w_out, preferred_element_type=jnp.float32)
    mixed = lax.psum(partial_out, "tensor")
    activations = (
        resid + mixed.reshape(count, patches, width) + bias_out.astype(jnp.float32)
    ).astype(jnp.bfloat16)
    dout_rows = cotangent.reshape(rows, width)
    d_hidden = contract(dout_rows, w_out, 1, 1)
    smooth_value, smooth_back = jax.vjp(smooth, chan_pre)
    d_pre = smooth_back(d_hidden)[0].astype(jnp.bfloat16)
    d_chan_part = contract(d_pre, w_in, 1, 1)
    d_chan = lax.psum(d_chan_part, "tensor")
    d_resid_norm, d_gain_two, d_shift_two = second_back(d_chan.reshape(count, patches, width))
    d_resid = cotangent.astype(jnp.float32) + d_resid_norm
    d_mixed = d_resid.astype(jnp.bfloat16)
    d_tokhid = jnp.einsum("sk,nsd->nkd", tok_second, d_mixed, preferred_element_type=jnp.float32)
    tok_value, tok_back = jax.vjp(smooth, tok_pre)
    d_tokpre = tok_back(d_tokhid)[0].astype(jnp.bfloat16)
    grad_second = jnp.einsum("nsd,nkd->sk", d_mixed, tok_hidden, preferred_element_type=jnp.float32)
    grad_first = jnp.einsum("nsd,nkd->sk", normed_low, d_tokpre, preferred_element_type=jnp.float32)
    grad_tbias = jnp.sum(d_tokpre, axis=(0, 2), dtype=jnp.float32)[None, :]
    grad_tbias_out = jnp.sum(d_mixed, axis=(0, 2), dtype=jnp.float32)
    d_normed = jnp.einsum("sk,nkd->nsd", tok_first, d_tokpre, preferred_element_type=jnp.float32)
    d_input_norm, d_gain_one, d_shift_one = first_back(d_normed)
    input_grad = (d_resid + d_input_norm).astype(jnp.bfloat16)
    grad_win = contract(chan_in, d_pre, 0, 0)
    grad_wout_t = contract(dout_rows, hidden, 0, 0)
    grad_bin = jnp.sum(d_pre, axis=0, dtype=jnp.float32)
    grad_bout = jnp.sum(dout_rows, axis=0, dtype=jnp.float32)
    share_win, share_wout_t, share_bin, share_bout = (
        lax.psum_scatter(grad_win, "dp", scatter_dimension=0, tiled=True),
        lax.psum_scatter(grad_wout_t, "dp", scatter_dimension=0, tiled=True),
        lax.psum_scatter(grad_bin, "dp", scatter_dimension=0, tiled=True),
        lax.psum_scatter(grad_bout, "dp", scatter_dimension=0, tiled=True),
    )
    share_gains, share_shifts, share_first, share_second, share_tbias = (
        lax.psum_scatter(
            jnp.stack([d_gain_one, d_gain_two]), "dp", scatter_dimension=1, tiled=True
        ),
        lax.psum_scatter(
            jnp.stack([d_shift_one, d_shift_two]), "dp", scatter_dimension=1, tiled=True
        ),
        lax.psum_scatter(grad_first, "dp", scatter_dimension=1, tiled=True),
        lax.psum_scatter(grad_second, "dp", scatter_dimension=1, tiled=True),
        lax.psum_scatter(grad_tbias, "dp", scatter_dimension=1, tiled=True),
    )
    total_tbias_out = lax.psum(grad_tbias_out, "dp")
    chan_cube = chan_in.reshape(count, patches, width)
    pre_cube = d_pre.reshape(count, patches, -1)
    hidden_cube = hidden.reshape(count, patches, -1)
    own_in = jnp.einsum("nsd,nsh->ndh", chan_cube, pre_cube, preferred_element_type=jnp.float32)
    own_out = jnp.einsum("nsd,nsh->ndh", cotangent, hidden_cube, preferred_element_type=jnp.float32)
    squares = jnp.sum(own_in * own_in, axis=(1, 2)) + jnp.sum(own_out * own_out, axis=(1, 2))
    train_in = own_in[QRY_DEV:]
    train_out = own_out[QRY_DEV:]
    query_chan = lax.all_gather(chan_cube[:QRY_DEV], "dp", axis=0, tiled=True)
    query_pre = lax.all_gather(pre_cube[:QRY_DEV], "dp", axis=0, tiled=True)
    query_hidden = lax.all_gather(hidden_cube[:QRY_DEV], "dp", axis=0, tiled=True)
    query_dout = lax.all_gather(cotangent[:QRY_DEV], "dp", axis=0, tiled=True)
    query_in = jnp.einsum("qsd,qsh->qdh", query_chan, query_pre, preferred_element_type=jnp.float32)
    query_out = jnp.einsum(
        "qsd,qsh->qdh", query_dout, query_hidden, preferred_element_type=jnp.float32
    )
    values = jnp.einsum("qab,tab->qt", query_in, train_in, precision=HIGH) + jnp.einsum(
        "qab,tab->qt", query_out, train_out, precision=HIGH
    )
    influence = values
    influence, squares = lax.psum((influence, squares), "tensor")
    sqnorms = squares / (2.0 * D * FF)
    influence = influence * (2.0 * D * FF) ** (-0.5)
    return (
        activations,
        input_grad,
        share_gains,
        share_shifts,
        share_first,
        share_second,
        share_tbias,
        total_tbias_out,
        share_win,
        share_bin,
        share_wout_t.T,
        share_bout,
        sqnorms,
        influence,
    )


def solution(mesh):
    placed = (
        P("dp", None, None),
        P("dp", None, None),
        P(None, "dp"),
        P(None, "dp"),
        P(None, "dp"),
        P(None, "dp"),
        P(None, "dp"),
        P(),
        P(None, "tensor"),
        P("tensor"),
        P("tensor", None),
        P(),
    )
    return jax.shard_map(
        per_device,
        mesh=mesh,
        in_specs=placed,
        out_specs=(
            P("dp", None, None),
            P("dp", None, None),
            P(None, "dp"),
            P(None, "dp"),
            P(None, "dp"),
            P(None, "dp"),
            P(None, "dp"),
            P(),
            P("dp", "tensor"),
            P(("tensor", "dp")),
            P("tensor", "dp"),
            P("dp"),
            P("dp"),
            P(None, "dp"),
        ),
        check_vma=False,
    )
```

profile of v0, /device:TPU:0, one launch (start us, length us, event | category | flops | bytes accessed | tf_op | source)
XLA Modules:
  0.0 650.8 jit_solution(5866668803341777422)
XLA Ops:
  8.1 10.9 %all_gather.31 = bf16[196,384]{0,1:T(8,128)(2,1)S(1)} all-gather(bf16[196,48]{0,1:T(8,128)(2,1)} %param.17), channel_id=1, replica_groups=mesh['dp'=8,'tensor'=4] {'dp'}, dimensions={1}, use_global_device_ids=true | all-gather | bytes 169344 | tf_op jit(solution)/shard_map/all_gather | solution.py:48
  19.0 8.5 %all-gather.3 = bf16[8,96,2]{1,2,0:T(2,128)(2,1)S(1)} all-gather(bf16[1,96,2]{1,2,0:T(2,128)(2,1)} %bitcast.137), channel_id=1, replica_groups=mesh['dp'=8,'tensor'=4] {'dp'}, dimensions={0}, use_global_device_ids=true | all-gather | bytes 3456 | tf_op jit(solution)/shard_map/all_gather | solution.py:46
  27.6 8.0 %all-gather.2 = bf16[8,96,2]{1,2,0:T(2,128)(2,1)S(1)} all-gather(bf16[1,96,2]{1,2,0:T(2,128)(2,1)} %bitcast.138), channel_id=1, replica_groups=mesh['dp'=8,'tensor'=4] {'dp'}, dimensions={0}, use_global_device_ids=true | all-gather | bytes 3456 | tf_op jit(solution)/shard_map/all_gather | solution.py:45
  37.5 9.1 %all_gather.29 = bf16[196,384]{0,1:T(8,128)(2,1)S(1)} all-gather(bf16[196,48]{0,1:T(8,128)(2,1)S(1)} %copy-done.19), channel_id=1, replica_groups=mesh['dp'=8,'tensor'=4] {'dp'}, dimensions={1}, use_global_device_ids=true | all-gather | bytes 169344 | tf_op jit(solution)/shard_map/all_gather | solution.py:47
  48.0 13.2 %all-reduce = bf16[384]{0:T(512)(128)(2,1)S(1)} all-reduce(bf16[384]{0:T(512)(128)(2,1)S(1)} %dynamic-update-slice), channel_id=1, replica_groups=mesh['dp'=8,'tensor'=4] {'dp'}, use_global_device_ids=true, to_apply=%add | all-reduce | flops 384 | bytes 1536
  72.6 2.9 convert_reduce_fusion.4
  78.5 2.8 reshape.127
  81.3 3.4 fusion.59
  85.4 137.2 %all-reduce.8.cloned.1.call-done = (f32[3,196,768]{2,1,0:T(8,128)}, f32[588,768]{1,0:T(8,128)}) async-done(((f32[3,196,768]{2,1,0:T(8,128)}, f32[588,768]{1,0:T(8,128)}), (f32[3,196,768]{2,1,0:T(8,128)}, f32[588,768]{1,0:T(8,128)})) %all-reduce.8.cloned.1.call-update) | async-done | bytes 3612688 | tf_op jit(solution)/shard_map/psum | solution.py:75
  225.3 2.9 multiply_reduce_fusion.2
  228.5 3.3 fusion.54
  234.8 3.2 convert_reduce_fusion
  252.9 4.0 fusion.60
  257.0 4.0 convolution_bitcast_fusion.2
  261.0 3.0 copy.74
  277.7 8.2 %copy.62 = f32[2,768,768]{2,0,1:T(2,128)} copy(f32[2,768,768]{1,2,0:T(8,128)} %slice.56) | data formatting | bytes 9437184 | tf_op jit(solution)/shard_map/slice | solution.py:127
  286.5 3.9 convert_reduce_fusion.2
  290.5 14.7 %all-reduce.3 = (f32[196]{0:T(256)}, f32[768]{0:T(1024)S(1)}, f32[768]{0:T(1024)S(1)}) all-reduce(f32[196]{0:T(256)S(1)} %get-tuple-element.87, f32[768]{0:T(1024)S(1)} %get-tuple-element.85, f32[768]{0:T(1024)S(1)} %get-tuple-element.93), channel_id=1, replica_groups=mesh['dp'=8,'tensor'=4] {'dp'}, use_global_device_ids=true, to_apply=%region_21.0 | all-reduce | flops 1732 | bytes 13856 | tf_op jit(solution)/shard_map/psum | solution.py:119
  306.4 3.3 convolution_bitcast_fusion.4
  309.8 4.3 convolution_bitcast_fusion.3
  317.0 26.5 %all-gather.17.cloned.1.call-done = bf16[8,196,768]{2,1,0:T(8,128)(2,1)} async-done(((bf16[1,196,768]{2,1,0:T(8,128)(2,1)}), bf16[8,196,768]{2,1,0:T(8,128)(2,1)}) %all-gather.17.cloned.1.call-update) | async-done | bytes 2408464 | tf_op jit(solution)/shard_map/all_gather | solution.py:130
  343.5 31.3 %all-gather.13.cloned.1.call-done = bf16[8,196,768]{2,1,0:T(8,128)(2,1)} async-done(((bf16[1,196,768]{2,1,0:T(8,128)(2,1)}), bf16[8,196,768]{2,1,0:T(8,128)(2,1)}) %all-gather.13.cloned.1.call-update) | async-done | bytes 2408464 | tf_op jit(solution)/shard_map/all_gather | solution.py:131
  374.8 11.7 %convolution_bitcast_fusion = f32[8,768,768]{1,2,0:T(8,128)} fusion(bf16[8,196,768]{2,1,0:T(8,128)(2,1)} %all-gather.17.cloned.1.call-done, bf16[8,196,768]{2,1,0:T(8,128)(2,1)} %all-gather.13.cloned.1.call-done), kind=kOutput, calls=%fused_computation.2 | convolution fusion | flops 1849688064 | bytes 23691264 | tf_op jit(solution)/shard_map/qsd,qsh->qdh/dot_general | solution.py:133
  386.5 19.5 %copy.61 = f32[8,768,768]{2,0,1:T(8,128)} copy(f32[8,768,768]{1,2,0:T(8,128)} %convolution_bitcast_fusion) | data formatting | bytes 37748736 | tf_op jit(solution)/shard_map/qsd,qsh->qdh/dot_general | solution.py:133
  406.2 31.5 %all-gather.15.cloned.1.call-done = bf16[8,196,768]{2,1,0:T(8,128)(2,1)} async-done(((bf16[1,196,768]{2,1,0:T(8,128)(2,1)}), bf16[8,196,768]{2,1,0:T(8,128)(2,1)}) %all-gather.15.cloned.1.call-update) | async-done | bytes 2408464 | tf_op jit(solution)/shard_map/all_gather | solution.py:129
  437.7 5.2 fusion.61
  442.9 44.7 %fusion.33 = f32[8,2]{0,1:T(2,128)S(1)} fusion(f32[2,768,768]{2,1,0:T(8,128)} %slice.54, f32[8,768,768]{2,1,0:T(8,128)S(1)} %fusion.61), kind=kOutput, calls=%fused_computation.65 | convolution fusion | flops 113246208 | bytes 23593024 | tf_op jit(solution)/shard_map/qab,tab->qt/dot_general | solution.py:136
  487.5 44.0 %fusion.38 = f32[8,2]{0,1:T(2,128)S(1)} fusion(f32[8,2]{0,1:T(2,128)S(1)} %fusion.33, f32[8,768,768]{2,0,1:T(8,128)} %copy.61, f32[2,768,768]{2,0,1:T(2,128)} %copy.62), kind=kOutput, calls=%fused_computation.67 | convolution fusion | flops 113246224 | bytes 23593088 | tf_op jit(solution)/shard_map/qab,tab->qt/dot_general | solution.py:136
  533.0 11.7 %all-reduce.4 = (f32[3]{0:T(128)S(1)}, f32[8,2]{0,1:T(2,128)S(1)}) all-reduce(f32[3]{0:T(128)S(1)} %add.168, f32[8,2]{0,1:T(2,128)S(1)} %fusion.38), channel_id=1, replica_groups=mesh['dp'=8,'tensor'=4] {'tensor'}, use_global_device_ids=true, to_apply=%region_30.0 | all-reduce | flops 19 | bytes 152 | tf_op jit(solution)/shard_map/psum | solution.py:140
  545.8 22.3 %reduce-scatter.28.cloned.1.call-done = f32[96,768]{1,0:T(8,128)} async-done(((f32[768,768]{1,0:T(8,128)}), f32[96,768]{1,0:T(8,128)}) %reduce-scatter.28.cloned.1.call-update) | async-done | bytes 294928
  568.1 37.8 %reduce-scatter.16.cloned.1.call-done = f32[196,48]{0,1:T(8,128)} async-done(((f32[196,384]{0,1:T(8,128)}), f32[196,48]{0,1:T(8,128)}) %reduce-scatter.16.cloned.1.call-update) | async-done | bytes 37648 | tf_op jit(solution)/shard_map/reduce_scatter | solution.py:115
  605.8 37.6 %reduce-scatter.18.cloned.1.call-done = f32[196,48]{0,1:T(8,128)} async-done(((f32[196,384]{0,1:T(8,128)}), f32[196,48]{0,1:T(8,128)}) %reduce-scatter.18.cloned.1.call-update) | async-done | bytes 37648 | tf_op jit(solution)/shard_map/reduce_scatter | solution.py:116
  (140 shorter events, 59.8 us)
Async XLA Ops:
  7.2 65.4 %copy-start = (bf16[768,768]{1,0:T(8,128)(2,1)S(1)}, bf16[768,768]{1,0:T(8,128)(2,1)}, u32[]{:S(2)}) copy-start(bf16[768,768]{1,0:T(8,128)(2,1)} %param.22) | copy-start | bytes 3538948
  7.2 39.3 %copy-start.22 = (u32[32]{0:T(128)S(1)}, u32[32]{0:T(128)}, u32[]{:S(2)}) copy-start(u32[32]{0:T(128)} %constant.43) | copy-start | bytes 388
  7.2 29.8 %copy-start.2 = (bf16[3,196,768]{2,1,0:T(8,128)(2,1)S(1)}, bf16[3,196,768]{2,1,0:T(8,128)(2,1)}, u32[]{:S(2)}) copy-start(bf16[3,196,768]{2,1,0:T(8,128)(2,1)} %param.12) | copy-start | bytes 2709508
  7.2 30.2 %copy-start.19 = (bf16[196,48]{0,1:T(8,128)(2,1)S(1)}, bf16[196,48]{0,1:T(8,128)(2,1)}, u32[]{:S(2)}) copy-start(bf16[196,48]{0,1:T(8,128)(2,1)} %param.16) | copy-start | bytes 56452
  7.2 40.6 %copy-start.23 = (bf16[1,48]{1,0:T(2,128)(2,1)S(1)}, bf16[1,48]{1,0:T(2,128)(2,1)}, u32[]{:S(2)}) copy-start(bf16[1,48]{1,0:T(2,128)(2,1)} %param.18) | copy-start | bytes 292
  7.2 215.4 %all-reduce.8.cloned.1.call-start = ((), (), s32[]{:S(2)}) async-start(), calls=%async_computation.18 | async-start | bytes 7323648 | tf_op jit(solution)/shard_map/psum | solution.py:75
  62.6 1.8 copy-start.11
  64.3 1.3 copy-start.4
  65.6 3.4 copy-start.20
  65.6 3.4 copy-start.6
  70.1 2.5 copy-start.18
  78.5 2.8 copy-start.15
  84.7 229.4 %reduce-scatter.26.cloned.1.call-start = ((), (), s32[]{:S(2)}) async-start(), calls=%async_computation.16 | async-start | bytes 221184
  225.3 2.9 copy-start.5
  225.3 3.2 copy-start.8
  231.7 1.2 copy-start.7
  231.8 3.0 copy-start.12
  233.0 5.0 copy-start.16
  241.3 4.6 copy-start.9
  242.2 73.3 %reduce-scatter.22.cloned.1.call-start = ((), (), s32[]{:S(2)}) async-start(), calls=%async_computation.14 | async-start | bytes 442368
  243.2 100.3 %all-gather.17.cloned.1.call-start = ((), (), s32[]{:S(2)}) async-start(), calls=%async_computation.13 | async-start | bytes 2764800 | tf_op jit(solution)/shard_map/all_gather | solution.py:130
  245.0 129.8 %all-gather.13.cloned.1.call-start = ((), (), s32[]{:S(2)}) async-start(), calls=%async_computation.11 | async-start | bytes 2764800 | tf_op jit(solution)/shard_map/all_gather | solution.py:131
  245.9 160.3 %all-gather.11.cloned.1.call-start = ((), (), s32[]{:S(2)}) async-start(), calls=%async_computation.10 | async-start | bytes 2764800 | tf_op jit(solution)/shard_map/all_gather | solution.py:128
  246.7 191.0 %all-gather.15.cloned.1.call-start = ((), (), s32[]{:S(2)}) async-start(), calls=%async_computation.12 | async-start | bytes 2764800 | tf_op jit(solution)/shard_map/all_gather | solution.py:129
  248.5 283.1 %reduce-scatter.24.cloned.1.call-start = ((), (), s32[]{:S(2)}) async-start(), calls=%async_computation.15 | async-start | bytes 442368
  252.9 292.9 %reduce-scatter.20.cloned.1.call-start = ((), (), s32[]{:S(2)}) async-start(), calls=%async_computation.9 | async-start | bytes 2654208 | tf_op jit(solution)/shard_map/reduce_scatter | solution.py:103
  257.0 311.1 %reduce-scatter.28.cloned.1.call-start = ((), (), s32[]{:S(2)}) async-start(), calls=%async_computation.17 | async-start | bytes 2654208
  264.1 341.8 %reduce-scatter.16.cloned.1.call-start = ((), (), s32[]{:S(2)}) async-start(), calls=%async_computation.7 | async-start | bytes 442368 | tf_op jit(solution)/shard_map/reduce_scatter | solution.py:115
  271.3 2.5 copy-start.10
  306.4 3.4 copy-start.17
  309.7 333.7 %reduce-scatter.18.cloned.1.call-start = ((), (), s32[]{:S(2)}) async-start(), calls=%async_computation.8 | async-start | bytes 442368 | tf_op jit(solution)/shard_map/reduce_scatter | solution.py:116
  487.5 155.9 %copy-start.1 = (bf16[768,768]{1,0:T(8,128)(2,1)S(1)}, bf16[768,768]{1,0:T(8,128)(2,1)}, u32[]{:S(2)}) copy-start(bf16[768,768]{1,0:T(8,128)(2,1)} %param.22) | copy-start | bytes 3538948
  (4 other events, 4.0 us)
Sparse Core Ops, SparseCore 0:
  84.9 137.6 all-reduce.7
  242.3 32.5 reduce-scatter.25
  278.2 33.8 reduce-scatter.21
  314.0 29.4 all-gather.16
  345.4 29.4 all-gather.12
  376.7 29.4 all-gather.10
  408.2 29.4 all-gather.14
  441.0 33.8 reduce-scatter.23
  479.3 42.4 reduce-scatter.19
  525.5 42.4 reduce-scatter.27
  572.0 33.7 reduce-scatter.15
  609.6 33.8 reduce-scatter.17
where the time goes:
time: 660 us; the launch traced here: 651 us
  waiting for transfers between devices  325 us (49%)
  matrix products  143 us (22%)
  blocking collectives  76 us (12%)
  local copies, waits for them, and re-layouts  69.3 us (10%)
  other arithmetic  20.2 us (3%)
  between operations  16.3 us (2%)
    psum x1, waiting for transfers between devices, per_device(): mixed = lax.psum(partial_out, 'tensor')  137 us
    dot_general x1, matrix products, per_device(): jnp.einsum('qab,tab->qt', query_in, train_in, precision=HIGH)  44.7 us
    dot_general x1, matrix products, per_device(): jnp.einsum('qab,tab->qt', query_out, train_out, precision=HIGH)  44 us
    reduce_scatter x1, waiting for transfers between devices, per_device(): lax.psum_scatter(grad_first, 'dp', scatter_dimension=1, tiled=True)  37.8 us
    reduce_scatter x1, waiting for transfers between devices, per_device(): lax.psum_scatter(grad_second, 'dp', scatter_dimension=1, tiled=True)  37.6 us
    all_gather x1, waiting for transfers between devices, per_device(): query_pre = lax.all_gather(pre_cube[:QRY_DEV], 'dp', axis=0, tiled=True)  31.5 us
    all_gather x1, waiting for transfers between devices, per_device(): query_dout = lax.all_gather(cotangent[:QRY_DEV], 'dp', axis=0, tiled=True)  31.3 us
    all_gather x1, waiting for transfers between devices, per_device(): lax.all_gather(hidden_cube[:QRY_DEV], 'dp', axis=0, tiled=True)  26.5 us
  transfers between devices with their start and end apart: 12, of which 8 were waited for; matrix products, arithmetic and copies ran while one was open for 29% of the time, Pallas kernels for 0%

commit v1 on v0

--- a/solution.py
+++ b/solution.py
@@ -1,14 +1,893 @@
+import functools
+
 import jax
 import jax.numpy as jnp
 from jax import lax
+from jax.experimental import pallas as pl
+from jax.experimental.pallas import tpu as pltpu
 from jax.sharding import PartitionSpec as P
 
 D = 768
 FF = 3072
 QRY_DEV = 1
-
-
 HIGH = lax.Precision.HIGHEST
+MESH = pl.DeviceIdType.MESH
+F32 = jnp.float32
+BF16 = jnp.bfloat16
+
+ROWS = 208
+CHUNK = 48
+LAG = 2
+C1 = 0.7978845608028654
+C2 = 0.044715
+
+
+def dot_nn(a, b):
+    return lax.dot_general(a, b, (((1,), (0,)), ((), ())), preferred_element_type=F32)
+
+
+def dot_nt(a, b):
+    return lax.dot_general(a, b, (((1,), (1,)), ((), ())), preferred_element_type=F32)
+
+
+def dot_tn(a, b):
+    return lax.dot_general(a, b, (((0,), (0,)), ((), ())), preferred_element_type=F32)
+
+
+def gelu_pair(v):
+    u = v * v
+    th = jnp.tanh(v * (C1 + (C1 * C2) * u))
+    hp = 0.5 + 0.5 * th
+    value = v * hp
+    slope = hp + (0.5 * v) * (1.0 - th * th) * (C1 + (3.0 * C1 * C2) * u)
+    return value, slope
+
+
+def fold(v):
+    out = v[0:8]
+    for s in range(8, v.shape[0], 8):
+        out = out + v[s : s + 8]
+    return out
+
+
+def mega(
+    n_dp,
+    count,
+    patches,
+    toks,
+    images,
+    cotangent,
+    w_in_h,
+    w_out_h,
+    gains_r,
+    shifts_r,
+    tok_in_r,
+    tok_out_r,
+    tok_bias_r,
+    tok_bias_out_r,
+    bias_in_r,
+    bias_out_r,
+    act_o,
+    ing_o,
+    gwi_o,
+    gwo_o,
+    gti_o,
+    gto_o,
+    vec_o,
+    tbo_o,
+    sm_o,
+    x_raw,
+    d_raw,
+    w_in,
+    w_out,
+    act_s,
+    ing_s,
+    pb,
+    aug,
+    misc,
+    toki_t,
+    toko_t,
+    toki,
+    toko,
+    gs,
+    dout,
+    dhid,
+    xf,
+    xh1,
+    rs1,
+    xh2,
+    rs2,
+    normed,
+    th,
+    tgp,
+    chan,
+    hid,
+    dpre,
+    tmp,
+    dq,
+    cq,
+    hq,
+    pq,
+    infl,
+    sqs,
+    dmix,
+    dtok,
+    dnorm,
+    zpart,
+    zrx,
+    zpair,
+    zrxp,
+    ztot,
+    gw,
+    wsib_s,
+    wsib_r,
+    wch_s,
+    wch_r,
+    gtok,
+    tsib_s,
+    tsib_r,
+    tch_s,
+    tch_r,
+    acc,
+    vec,
+    vsib_r,
+    vch,
+    zsm,
+    in_sem,
+    out_sem,
+    pb_c,
+    pb_x,
+    dq_c,
+    dq_x,
+    cq_c,
+    cq_x,
+    ze,
+    zm,
+    zt,
+    w_sem,
+    t_sem,
+    v_sem,
+    s_sem,
+):
+    me = lax.axis_index("dp")
+    t = lax.axis_index("tensor")
+    core = me % 2
+    chip = me // 2
+    sib = chip * 2 + 1 - core
+    nc = n_dp // 2
+    mid = (t == 1) | (t == 2)
+    end = (t == 0) | (t == 3)
+    end_peer = jnp.where(t < 2, 1, 2)
+    mid_end = jnp.where(t < 2, 0, 3)
+    mid_peer = 3 - t
+    shard = D // n_dp
+    ks = toks // n_dp
+    kb = -(-ks // 16) * 16
+    K = n_dp * kb
+    KA = K + 16
+    R = count * ROWS
+    half = R // CHUNK
+    steps = 2 * half
+    nblk = ROWS // 16
+    last = ROWS - 16
+    tail = patches - last
+
+    def peer(k):
+        return ((chip + k) % nc) * 2 + core
+
+    def src(k):
+        return ((chip - k + nc) % nc) * 2 + core
+
+    def src_sib(k):
+        return ((chip - k + nc) % nc) * 2 + 1 - core
+
+    def rcopy(a, b, ss, rs, dev):
+        return pltpu.make_async_remote_copy(
+            src_ref=a, dst_ref=b, send_sem=ss, recv_sem=rs, device_id=dev, device_id_type=MESH
+        )
+
+    class Gather:
+        def __init__(self, buf, c, x):
+            self.buf, self.c, self.x = buf, c, x
+
+        def chip_copy(self, k):
+            return rcopy(
+                self.buf.at[me], self.buf.at[me], self.c.at[0, k - 1], self.c.at[1, k - 1], (peer(k), t)
+            )
+
+        def sib_copy(self, k):
+            s = src(k)
+            return rcopy(self.buf.at[s], self.buf.at[s], self.x.at[0, k], self.x.at[1, k], (sib, t))
+
+        def start(self):
+            for k in range(1, nc):
+                self.chip_copy(k).start()
+            self.sib_copy(0).start()
+
+        def relay(self, k):
+            s = src(k)
+            rcopy(
+                self.buf.at[s], self.buf.at[s], self.c.at[0, k - 1], self.c.at[1, k - 1], (sib, t)
+            ).wait_recv()
+            self.sib_copy(k).start()
+
+        def from_sib(self, k):
+            s = src_sib(k)
+            rcopy(
+                self.buf.at[s], self.buf.at[s], self.x.at[0, k], self.x.at[1, k], (sib, t)
+            ).wait_recv()
+
+        def drain(self):
+            for k in range(1, nc):
+                self.chip_copy(k).wait_send()
+            for k in range(nc):
+                self.sib_copy(k).wait_send()
+
+    params = Gather(pb, pb_c, pb_x)
+    dqs = Gather(dq, dq_c, dq_x)
+    cqs = Gather(cq, cq_c, cq_x)
+
+    loads = [
+        pltpu.make_async_copy(cotangent, d_raw, in_sem.at[0]),
+        pltpu.make_async_copy(w_out_h, w_out, in_sem.at[1]),
+        pltpu.make_async_copy(images, x_raw, in_sem.at[2]),
+        pltpu.make_async_copy(w_in_h, w_in, in_sem.at[3]),
+    ]
+    for c in loads:
+        c.start()
+
+    barrier = pltpu.get_barrier_semaphore()
+    others = [(sib, t)] + [(peer(k), t) for k in range(1, nc)] + [(me, (t + k) % 4) for k in (1, 2, 3)]
+    for dev in others:
+        pl.semaphore_signal(barrier, inc=1, device_id=dev, device_id_type=MESH)
+
+    pb[me] = jnp.zeros(pb.shape[1:], BF16)
+    eye = (
+        lax.broadcasted_iota(jnp.int32, (kb, 128), 0) == lax.broadcasted_iota(jnp.int32, (kb, 128), 1)
+    ).astype(BF16)
+    aug[...] = jnp.zeros(aug.shape, F32)
+    aug[0:patches, 0:ks] = tok_in_r[...].astype(F32)
+    aug[patches : patches + 1, 0:ks] = tok_bias_r[...].astype(F32)
+    pb[me, 0:kb, 0:ROWS] = dot_nt(eye, aug[...].astype(BF16)).astype(BF16)
+    aug[0:patches, 0:ks] = tok_out_r[...].astype(F32)
+    aug[patches : patches + 1, 0:ks] = jnp.zeros((1, ks), F32)
+    pb[me, kb : 2 * kb, 0:ROWS] = dot_nt(eye, aug[...].astype(BF16)).astype(BF16)
+    misc[...] = jnp.zeros(misc.shape, F32)
+    misc[0:2, 0:shard] = gains_r[...].astype(F32)
+    misc[2:4, 0:shard] = shifts_r[...].astype(F32)
+    pb[me, 2 * kb : 2 * kb + 16, :] = misc[...].astype(BF16)
+
+    pl.semaphore_wait(barrier, len(others))
+    params.start()
+
+    loads[0].wait()
+    misc[...] = jnp.zeros(misc.shape, F32)
+    acc[...] = jnp.zeros(acc.shape, F32)
+
+    def pad_dout(i, carry):
+        base = pl.multiple_of(i * ROWS, 16)
+        dout[pl.ds(base, last), :] = d_raw[i, 0:last, :]
+        for c in range(0, D, 256):
+            misc[0:tail, :] = d_raw[i, last:patches, c : c + 256].astype(F32)
+            dout[pl.ds(base + last, 16), c : c + 256] = misc[...].astype(BF16)
+        a = jnp.zeros((8, D), F32)
+        for b in range(nblk):
+            a = a + fold(dout[pl.ds(base + 16 * b, 16), :].astype(F32))
+        acc[4] += a
+        return carry
+
+    lax.fori_loop(0, count, pad_dout, 0)
+    dq[me] = dout[0:ROWS, :]
+    dqs.start()
+
+    loads[1].wait()
+
+    def hidden_grad(i, carry):
+        r = pl.ds(pl.multiple_of(i * ROWS, 16), ROWS)
+        for c in range(0, D, 256):
+            dhid[r, c : c + 256] = dot_nt(dout[r, :], w_out[c : c + 256, :])
+        return carry
+
+    lax.fori_loop(0, count, hidden_grad, 0)
+
+    loads[2].wait()
+
+    def first_norm(i, carry):
+        base = pl.multiple_of(i * ROWS, 16)
+        xf[pl.ds(base + last, 16), :] = jnp.zeros((16, D), F32)
+        xf[pl.ds(base, last), :] = x_raw[i, 0:last, :].astype(F32)
+        xf[pl.ds(base + last, tail), :] = x_raw[i, last:patches, :].astype(F32)
+        for b in range(nblk):
+            r = pl.ds(base + 16 * b, 16)
+            v = xf[r, :]
+            center = v - jnp.mean(v, axis=-1, keepdims=True)
+            inv = lax.rsqrt(jnp.mean(center * center, axis=-1, keepdims=True) + 1e-06)
+            xh1[r, :] = center * inv
+            rs1[r, :] = jnp.broadcast_to(inv, (16, 128))
+        return carry
+
+    lax.fori_loop(0, count, first_norm, 0)
+
+    for k in range(1, nc):
+        params.relay(k)
+    for k in range(nc):
+        params.from_sib(k)
+    full = jnp.zeros((16, D), F32)
+    for d in range(n_dp):
+        toki_t[d * kb : (d + 1) * kb, :] = pb[d, 0:kb, :]
+        toko_t[d * kb : (d + 1) * kb, :] = pb[d, kb : 2 * kb, :]
+        part = pb[d, 2 * kb : 2 * kb + 16, 0:128].astype(F32)
+        part = jnp.concatenate([part, jnp.zeros((16, D - 128), F32)], axis=1)
+        full = full + (pltpu.roll(part, d * shard, 1) if d else part)
+    gs[...] = full
+    misc[...] = jnp.zeros(misc.shape, F32)
+    misc[0:1, 0:patches] = tok_bias_out_r[...].astype(F32)
+    toko_t[K:KA, :] = misc[...].astype(BF16)
+    ri = lax.broadcasted_iota(jnp.int32, (ROWS, ROWS), 0)
+    ci = lax.broadcasted_iota(jnp.int32, (ROWS, ROWS), 1)
+    eye_rows = ((ri == ci) & (ri < patches)).astype(BF16)
+    toki[:, 0:K] = dot_nt(eye_rows, toki_t[:, 0:ROWS]).astype(BF16)
+    toko[:, 0:KA] = dot_nt(eye_rows, toko_t[:, 0:ROWS]).astype(BF16)
+    loads[3].wait()
+
+    def zrows(c):
+        return pl.ds(pl.multiple_of(c * CHUNK, 16), CHUNK)
+
+    def up_copy(c):
+        return rcopy(zpart.at[zrows(c)], zrx.at[zrows(c)], ze.at[0, c], ze.at[1, c], (me, end_peer))
+
+    def mid_copy(c):
+        return rcopy(zpair.at[zrows(c)], zrxp.at[zrows(c)], zm.at[0, c], zm.at[1, c], (me, mid_peer))
+
+    def down_copy(c):
+        return rcopy(ztot.at[zrows(c)], ztot.at[zrows(c)], zt.at[0, c], zt.at[1, c], (me, mid_end))
+
+    def start_up(first, extra, more):
+        @pl.when(end)
+        def _():
+            for j in range(4):
+                up_copy(first + j).start()
+
+            @pl.when(more)
+            def _():
+                for j in range(4, 4 + extra):
+                    up_copy(first + j).start()
+
+    def zpair_step(c):
+        up_copy(c).wait_recv()
+        r = zrows(c)
+        zpair[r, :] = (zpart[r, :].astype(F32) + zrx[r, :].astype(F32)).astype(BF16)
+        mid_copy(c).start()
+
+    def ztot_step(c):
+        mid_copy(c).wait_recv()
+        r = zrows(c)
+        ztot[r, :] = (zpair[r, :].astype(F32) + zrxp[r, :].astype(F32)).astype(BF16)
+        down_copy(c).start()
+
+    def zslot(s):
+        @pl.when(mid)
+        def _():
+            if isinstance(s, int):
+                if s < steps:
+                    zpair_step(s)
+                if 0 <= s - LAG < steps:
+                    ztot_step(s - LAG)
+            else:
+                zpair_step(s)
+                ztot_step(s - LAG)
+
+    def zfin(first, number):
+        @pl.when(end)
+        def _():
+            for j in range(number):
+                down_copy(first + j).wait_recv()
+
+    def forward(i, carry):
+        base = pl.multiple_of(i * ROWS, 16)
+        r = pl.ds(base, ROWS)
+        for b in range(nblk):
+            rb = pl.ds(base + 16 * b, 16)
+            v = xh1[rb, :] * gs[0:1, :] + gs[2:3, :]
+            if 16 * (b + 1) > patches:
+                row = lax.broadcasted_iota(jnp.int32, (16, D), 0) + 16 * b
+                v = jnp.where(row < patches, v, jnp.where(row == patches, 1.0, 0.0))
+            normed[rb, :] = v.astype(BF16)
+        th[i, K:KA, :] = (lax.broadcasted_iota(jnp.int32, (16, D), 0) == 0).astype(F32).astype(BF16)
+        for c in range(0, D, 256):
+            tmp[0:K, :] = dot_nn(toki_t[:, 0:ROWS], normed[r, c : c + 256])
+            for b in range(0, K, 16):
+                value, slope = gelu_pair(tmp[b : b + 16, :])
+                th[i, b : b + 16, c : c + 256] = value.astype(BF16)
+                tgp[i, b : b + 16, c : c + 256] = slope
+            xf[r, c : c + 256] += dot_nn(toko[:, 0:KA], th[i, :, c : c + 256])
+        for b in range(nblk):
+            rb = pl.ds(base + 16 * b, 16)
+            v = xf[rb, :]
+            center = v - jnp.mean(v, axis=-1, keepdims=True)
+            inv = lax.rsqrt(jnp.mean(center * center, axis=-1, keepdims=True) + 1e-06)
+            xhat = center * inv
+            xh2[rb, :] = xhat
+            rs2[rb, :] = jnp.broadcast_to(inv, (16, 128))
+            chan[rb, :] = (xhat * gs[1:2, :] + gs[3:4, :]).astype(BF16)
+
+        @pl.when(i == 0)
+        def _():
+            cq[me] = chan[0:ROWS, :]
+            cqs.start()
+
+        for c in range(0, D, 256):
+            tmp[0:ROWS, :] = dot_nn(chan[r, :], w_in[:, c : c + 256])
+            a = jnp.zeros((8, 256), F32)
+            for b in range(nblk):
+                rb = pl.ds(base + 16 * b, 16)
+                value, slope = gelu_pair(tmp[16 * b : 16 * b + 16, :] + bias_in_r[:, c : c + 256])
+                hid[rb, c : c + 256] = value.astype(BF16)
+                low = (slope * dhid[rb, c : c + 256]).astype(BF16)
+                dpre[rb, c : c + 256] = low
+                a = a + fold(low.astype(F32))
+            acc[5, :, c : c + 256] += a
+        for c in range(0, D, 256):
+            zpart[r, c : c + 256] = dot_nt(dpre[r, :], w_in[c : c + 256, :]).astype(BF16)
+        start_up(4 * i, half - 4 * count, i == count - 1)
+        return carry
+
+    lax.fori_loop(0, count, forward, 0)
+
+    def partial_out(i, carry):
+        r = pl.ds(pl.multiple_of(i * ROWS, 16), ROWS)
+        ro = pl.ds(pl.multiple_of(R + i * ROWS, 16), ROWS)
+        for c in range(0, D, 256):
+            zpart[ro, c : c + 256] = dot_nn(hid[r, :], w_out[:, c : c + 256]).astype(BF16)
+        start_up(half + 4 * i, half - 4 * count, i == count - 1)
+        return carry
+
+    lax.fori_loop(0, count, partial_out, 0)
+    zslot(0)
+    zslot(1)
+
+    def weight_grad(j, carry):
+        cols = pl.ds(pl.multiple_of(j * 256, 256), 256)
+        gw[0, cols, :] = dot_tn(chan[:, cols], dpre[...])
+        gw[1, cols, :] = dot_tn(dout[:, cols], hid[...])
+        return carry
+
+    lax.fori_loop(0, D // 256, weight_grad, 0)
+    for c in range(nc):
+        rows = pl.ds(pl.multiple_of((2 * c + 1 - core) * shard, 8), shard)
+        for m in range(2):
+            wsib_s[c, m] = gw[m, rows, :].astype(BF16)
+    w_sib = rcopy(wsib_s, wsib_r, w_sem.at[0, 0], w_sem.at[1, 0], (sib, t))
+    w_sib.start()
+    zslot(2)
+
+    sqs[...] = jnp.zeros(sqs.shape, F32)
+
+    def square(i, carry):
+        r = pl.ds(pl.multiple_of(i * ROWS, 16), ROWS)
+        g1 = dot_nt(chan[r, :], chan[r, :]) * dot_nt(dpre[r, :], dpre[r, :])
+        g2 = dot_nt(dout[r, :], dout[r, :]) * dot_nt(hid[r, :], hid[r, :])
+        sqs[pl.ds(i, 1), 0:ROWS] = jnp.sum(g1 + g2, axis=0, keepdims=True)
+        return carry
+
+    lax.fori_loop(0, count, square, 0)
+    zslot(3)
+
+    w_sib.wait_recv()
+
+    def w_chip(k):
+        return rcopy(
+            wch_s.at[k - 1], wch_r.at[k - 1], w_sem.at[0, k], w_sem.at[1, k], (peer(k), t)
+        )
+
+    for k in range(1, nc):
+        dest = (chip + k) % nc
+        rows = pl.ds(pl.multiple_of((2 * dest + core) * shard, 8), shard)
+        for m in range(2):
+            wch_s[k - 1, m] = (gw[m, rows, :] + wsib_r[dest, m].astype(F32)).astype(BF16)
+        w_chip(k).start()
+    zslot(4)
+
+    infl[...] = jnp.zeros(infl.shape, F32)
+
+    def query(j, carry):
+        k = j // 2
+        own = j % 2 == 0
+        slot = jnp.where(own, src(k), src_sib(k))
+
+        @pl.when(own & (k > 0))
+        def _():
+            dqs.relay(k)
+            cqs.relay(k)
+
+        @pl.when(jnp.logical_not(own))
+        def _():
+            dqs.from_sib(k)
+            cqs.from_sib(k)
+
+        @pl.when(j + 5 < half)
+        def _():
+            zslot(j + 5)
+
+        for c in range(0, D, 256):
+            tmp[0:ROWS, :] = dot_nn(cq[slot], w_in[:, c : c + 256])
+            tmp[ROWS : 2 * ROWS, :] = dot_nt(dq[slot], w_out[c : c + 256, :])
+            for b in range(0, ROWS, 16):
+                value, slope = gelu_pair(tmp[b : b + 16, :] + bias_in_r[:, c : c + 256])
+                hq[b : b + 16, c : c + 256] = value.astype(BF16)
+                pq[b : b + 16, c : c + 256] = (slope * tmp[ROWS + b : ROWS + b + 16, :]).astype(BF16)
+        for q in range(count - QRY_DEV):
+            r = slice((QRY_DEV + q) * ROWS, (QRY_DEV + q + 1) * ROWS)
+            g1 = dot_nt(cq[slot], chan[r, :]) * dot_nt(pq[...], dpre[r, :])
+            g2 = dot_nt(dq[slot], dout[r, :]) * dot_nt(hq[...], hid[r, :])
+            infl[q, pl.ds(slot, 1), 0:ROWS] = jnp.sum(g1 + g2, axis=0, keepdims=True)
+        return carry
+
+    lax.fori_loop(0, n_dp, query, 0)
+    for s in range(min(n_dp + 5, half), half + LAG):
+        zslot(s)
+
+    lane = lax.broadcasted_iota(jnp.int32, (n_dp, 128), 1)
+    sm = jnp.zeros((n_dp, 128), F32)
+    for q in range(count - QRY_DEV):
+        sm = jnp.where(lane == q, jnp.sum(infl[q], axis=1, keepdims=True), sm)
+    zsm[t, 0:n_dp, :] = sm * (2.0 * D * FF) ** (-0.5)
+    zsm[t, n_dp : n_dp + 8, :] = jnp.broadcast_to(
+        jnp.sum(sqs[...], axis=1, keepdims=True) / (2.0 * D * FF), (8, 128)
+    )
+
+    def sm_copy(k):
+        return rcopy(
+            zsm.at[t], zsm.at[t], s_sem.at[0, k - 1], s_sem.at[1, k - 1], (me, (t + k) % 4)
+        )
+
+    for k in (1, 2, 3):
+        sm_copy(k).start()
+
+    gtok[...] = jnp.zeros(gtok.shape, F32)
+
+    def ing_copy(i):
+        return pltpu.make_async_copy(ing_s.at[i], ing_o.at[i], out_sem.at[0, i])
+
+    def backward(i, carry):
+        @pl.when(i == 0)
+        def _():
+            zfin(0, 1)
+
+        zfin(4 * i + 1, 4)
+        base = pl.multiple_of(i * ROWS, 16)
+        r = pl.ds(base, ROWS)
+        a1 = jnp.zeros((8, D), F32)
+        a3 = jnp.zeros((8, D), F32)
+        for b in range(nblk):
+            rb = pl.ds(base + 16 * b, 16)
+            e = ztot[rb, :].astype(F32)
+            xhat = xh2[rb, :]
+            a1 = a1 + fold(e * xhat)
+            a3 = a3 + fold(e)
+            eg = e * gs[1:2, :]
+            m1 = jnp.mean(eg, axis=-1, keepdims=True)
+            m2 = jnp.mean(eg * xhat, axis=-1, keepdims=True)
+            d = dout[rb, :].astype(F32) + rs2[rb, 0:1] * (eg - m1 - xhat * m2)
+            dhid[rb, :] = d
+            dmix[16 * b : 16 * b + 16, :] = d.astype(BF16)
+        acc[1] += a1
+        acc[3] += a3
+        for c in range(0, D, 256):
+            tmp[0:K, :] = dot_nn(toko_t[0:K, 0:ROWS], dmix[:, c : c + 256])
+            for b in range(0, K, 16):
+                dtok[b : b + 16, c : c + 256] = (
+                    tmp[b : b + 16, :] * tgp[i, b : b + 16, c : c + 256]
+                ).astype(BF16)
+        gtok[0, 0:K, 0:ROWS] += dot_nt(dtok[...], normed[r, :])
+        gtok[1, :, 0:ROWS] += dot_nt(th[i], dmix[...])
+        for c in range(0, D, 256):
+            dnorm[:, c : c + 256] = dot_nn(toki[:, 0:K], dtok[:, c : c + 256])
+        a0 = jnp.zeros((8, D), F32)
+        a2 = jnp.zeros((8, D), F32)
+        for b in range(nblk):
+            rb = pl.ds(base + 16 * b, 16)
+            e = dnorm[16 * b : 16 * b + 16, :]
+            xhat = xh1[rb, :]
+            a0 = a0 + fold(e * xhat)
+            a2 = a2 + fold(e)
+            eg = e * gs[0:1, :]
+            m1 = jnp.mean(eg, axis=-1, keepdims=True)
+            m2 = jnp.mean(eg * xhat, axis=-1, keepdims=True)
+            d = (dhid[rb, :] + rs1[rb, 0:1] * (eg - m1 - xhat * m2)).astype(BF16)
+            n = min(16, patches - 16 * b)
+            ing_s[i, 16 * b : 16 * b + n, :] = d[0:n]
+        acc[0] += a0
+        acc[2] += a2
+        ing_copy(i).start()
+        zslot(half + LAG + i)
+        return carry
+
+    lax.fori_loop(0, count, backward, 0)
+    done = half + LAG + count
+
+    for c in range(nc):
+        rows = pl.ds(pl.multiple_of((2 * c + 1 - core) * kb, 8), kb)
+        for m in range(2):
+            tsib_s[c, m] = gtok[m, rows, :]
+    t_sib = rcopy(tsib_s, tsib_r, t_sem.at[0, 0], t_sem.at[1, 0], (sib, t))
+    t_sib.start()
+    vec[...] = jnp.zeros(vec.shape, F32)
+    for q in range(6):
+        vec[q : q + 1, :] = jnp.sum(acc[q], axis=0, keepdims=True)
+    vec[6:7, 0:256] = gtok[1, K : K + 1, :]
+    v_sib = rcopy(vec, vsib_r, v_sem.at[0, 0], v_sem.at[1, 0], (sib, t))
+    v_sib.start()
+    zslot(done)
+    v_sib.wait_recv()
+
+    def v_chip(k):
+        return rcopy(
+            vch.at[chip], vch.at[chip], v_sem.at[0, k], v_sem.at[1, k], (peer(k), t)
+        )
+
+    vch[chip] = vec[...] + vsib_r[...]
+    for k in range(1, nc):
+        v_chip(k).start()
+    t_sib.wait_recv()
+
+    def t_chip(k):
+        return rcopy(
+            tch_s.at[k - 1], tch_r.at[k - 1], t_sem.at[0, k], t_sem.at[1, k], (peer(k), t)
+        )
+
+    for k in range(1, nc):
+        dest = (chip + k) % nc
+        rows = pl.ds(pl.multiple_of((2 * dest + core) * kb, 8), kb)
+        for m in range(2):
+            tch_s[k - 1, m] = gtok[m, rows, :] + tsib_r[dest, m]
+        t_chip(k).start()
+    zslot(done + 1)
+
+    rows = pl.ds(pl.multiple_of(me * shard, 8), shard)
+    for m, out in enumerate((gwi_o, gwo_o)):
+        out[...] = gw[m, rows, :] + wsib_r[chip, m].astype(F32)
+    for k in range(1, nc):
+        w_chip(k).wait_recv()
+        for m, out in enumerate((gwi_o, gwo_o)):
+            out[...] += wch_r[k - 1, m].astype(F32)
+    zslot(done + 2)
+    zslot(done + 3)
+    for k in (1, 2, 3):
+        sm_copy(k).wait_recv()
+    sm_o[...] = (zsm[0] + zsm[1]) + (zsm[2] + zsm[3])
+    rows = pl.ds(pl.multiple_of(me * kb, 8), kb)
+    for m, out in enumerate((gti_o, gto_o)):
+        out[...] = gtok[m, rows, :] + tsib_r[chip, m]
+    for k in range(1, nc):
+        t_chip(k).wait_recv()
+        for m, out in enumerate((gti_o, gto_o)):
+            out[...] += tch_r[k - 1, m]
+    for k in range(1, nc):
+        v_chip(k).wait_recv()
+    total = vch[0]
+    for c in range(1, nc):
+        total = total + vch[c]
+    tbo_o[...] = total[:, 0:256]
+    vec_o[...] = pltpu.roll(total, (D - me * shard) % D, 1)[:, 0:128]
+
+    def act_copy(i):
+        return pltpu.make_async_copy(act_s.at[i], act_o.at[i], out_sem.at[1, i])
+
+    at = done + 4
+    for i in range(count):
+        need = -(-((i + 1) * ROWS) // CHUNK) + half
+        while at < min(need + LAG, steps + LAG):
+            zslot(at)
+            at += 1
+        first = half if i == 0 else -(-(i * ROWS) // CHUNK) + half
+        zfin(first, need - first)
+        for b in range(nblk):
+            n = min(16, patches - 16 * b)
+            rb = slice(i * ROWS + 16 * b, i * ROWS + 16 * b + 16)
+            ro = slice(R + i * ROWS + 16 * b, R + i * ROWS + 16 * b + 16)
+            a = (xf[rb, :] + ztot[ro, :].astype(F32) + bias_out_r[...]).astype(BF16)
+            act_s[i, 16 * b : 16 * b + n, :] = a[0:n]
+        act_copy(i).start()
+
+    params.drain()
+    dqs.drain()
+    cqs.drain()
+
+    def drain_end(c, carry):
+        up_copy(c).wait_send()
+        return carry
+
+    def drain_mid(c, carry):
+        mid_copy(c).wait_send()
+        down_copy(c).wait_send()
+        return carry
+
+    @pl.when(end)
+    def _():
+        lax.fori_loop(0, steps, drain_end, 0)
+
+    @pl.when(mid)
+    def _():
+        lax.fori_loop(0, steps, drain_mid, 0)
+
+    w_sib.wait_send()
+    t_sib.wait_send()
+    v_sib.wait_send()
+    for k in range(1, nc):
+        w_chip(k).wait_send()
+        t_chip(k).wait_send()
+        v_chip(k).wait_send()
+    for k in (1, 2, 3):
+        sm_copy(k).wait_send()
+    for i in range(count):
+        ing_copy(i).wait()
+        act_copy(i).wait()
+
+
+def fused(
+    n_dp,
+    images,
+    cotangent,
+    norm_gains,
+    norm_shifts,
+    tok_in,
+    tok_out_t,
+    tok_bias_in,
+    tok_bias_out,
+    w_in,
+    bias_in,
+    w_out,
+    bias_out,
+):
+    count, patches, width = images.shape
+    nc = n_dp // 2
+    ks = tok_in.shape[1]
+    toks = ks * n_dp
+    kb = -(-ks // 16) * 16
+    K = n_dp * kb
+    KA = K + 16
+    KL = -(-KA // 128) * 128
+    R = count * ROWS
+    steps = 2 * (R // CHUNK)
+    shard = width // n_dp
+    hidden = w_in.shape[1]
+    anyspace = pl.BlockSpec(memory_space=pl.ANY)
+    vm = pl.BlockSpec(memory_space=pltpu.VMEM)
+    V = pltpu.VMEM
+    dma = lambda *s: pltpu.SemaphoreType.DMA(s)
+    smr = n_dp + 8
+    scratch = dict(
+        x_raw=V((count, patches, D), BF16),
+        d_raw=V((count, patches, D), BF16),
+        w_in=V((D, hidden), BF16),
+        w_out=V((hidden, D), BF16),
+        act_s=V((count, patches, D), BF16),
+        ing_s=V((count, patches, D), BF16),
+        pb=V((n_dp, 2 * kb + 16, 256), BF16),
+        aug=V((ROWS, 128), F32),
+        misc=V((16, 256), F32),
+        toki_t=V((K, 256), BF16),
+        toko_t=V((KA, 256), BF16),
+        toki=V((ROWS, KL), BF16),
+        toko=V((ROWS, KL), BF16),
+        gs=V((16, D), F32),
+        dout=V((R, D), BF16),
+        dhid=V((R, hidden), F32),
+        xf=V((R, D), F32),
+        xh1=V((R, D), F32),
+        rs1=V((R, 128), F32),
+        xh2=V((R, D), F32),
+        rs2=V((R, 128), F32),
+        normed=V((R, D), BF16),
+        th=V((count, KA, D), BF16),
+        tgp=V((count, K, D), F32),
+        chan=V((R, D), BF16),
+        hid=V((R, hidden), BF16),
+        dpre=V((R, hidden), BF16),
+        tmp=V((max(K, 2 * ROWS), 256), F32),
+        dq=V((n_dp, ROWS, D), BF16),
+        cq=V((n_dp, ROWS, D), BF16),
+        hq=V((ROWS, hidden), BF16),
+        pq=V((ROWS, hidden), BF16),
+        infl=V((count - QRY_DEV, n_dp, 256), F32),
+        sqs=V((8, 256), F32),
+        dmix=V((ROWS, D), BF16),
+        dtok=V((K, D), BF16),
+        dnorm=V((ROWS, D), F32),
+        zpart=V((2 * R, D), BF16),
+        zrx=V((2 * R, D), BF16),
+        zpair=V((2 * R, D), BF16),
+        zrxp=V((2 * R, D), BF16),
+        ztot=V((2 * R, D), BF16),
+        gw=V((2, D, hidden), F32),
+        wsib_s=V((nc, 2, shard, hidden), BF16),
+        wsib_r=V((nc, 2, shard, hidden), BF16),
+        wch_s=V((nc - 1, 2, shard, hidden), BF16),
+        wch_r=V((nc - 1, 2, shard, hidden), BF16),
+        gtok=V((2, KA, 256), F32),
+        tsib_s=V((nc, 2, kb, 256), F32),
+        tsib_r=V((nc, 2, kb, 256), F32),
+        tch_s=V((nc - 1, 2, kb, 256), F32),
+        tch_r=V((nc - 1, 2, kb, 256), F32),
+        acc=V((6, 8, D), F32),
+        vec=V((8, D), F32),
+        vsib_r=V((8, D), F32),
+        vch=V((nc, 8, D), F32),
+        zsm=V((4, smr, 128), F32),
+        in_sem=dma(4),
+        out_sem=dma(2, count),
+        pb_c=dma(2, nc - 1),
+        pb_x=dma(2, nc),
+        dq_c=dma(2, nc - 1),
+        dq_x=dma(2, nc),
+        cq_c=dma(2, nc - 1),
+        cq_x=dma(2, nc),
+        ze=dma(2, steps),
+        zm=dma(2, steps),
+        zt=dma(2, steps),
+        w_sem=dma(2, nc),
+        t_sem=dma(2, nc),
+        v_sem=dma(2, nc),
+        s_sem=dma(2, 3),
+    )
+    outs = [
+        (images.shape, BF16, anyspace),
+        (images.shape, BF16, anyspace),
+        ((shard, hidden), F32, vm),
+        ((shard, hidden), F32, vm),
+        ((kb, 256), F32, vm),
+        ((kb, 256), F32, vm),
+        ((8, 128), F32, vm),
+        ((8, 256), F32, vm),
+        ((smr, 128), F32, vm),
+    ]
+    names = list(scratch)
+    n_in, n_out = 12, len(outs)
+
+    def body(*refs):
+        mega(n_dp, count, patches, toks, *refs[: n_in + n_out], **dict(zip(names, refs[n_in + n_out :])))
+
+    act, ing, gwi, gwo, gti, gto, vec, tbo, sm = pl.pallas_call(
+        body,
+        out_shape=[jax.ShapeDtypeStruct(s, d) for s, d, _ in outs],
+        in_specs=[anyspace] * 4 + [vm] * 8,
+        out_specs=[o[2] for o in outs],
+        scratch_shapes=list(scratch.values()),
+        compiler_params=pltpu.CompilerParams(
+            collective_id=0, has_side_effects=True, vmem_limit_bytes=60 * 2**20
+        ),
+        name="mixer",
+    )(
+        images,
+        cotangent,
+        w_in,
+        w_out,
+        norm_gains,
+        norm_shifts,
+        tok_in,
+        tok_out_t,
+        tok_bias_in,
+        tok_bias_out.reshape(1, -1),
+        bias_in.astype(F32).reshape(1, -1),
+        bias_out.astype(F32).reshape(1, -1),
+    )
+    return (
+        act,
+        ing,
+        vec[0:2, 0:shard],
+        vec[2:4, 0:shard],
+        gti[0:ks, 0:patches].T,
+        gto[0:ks, 0:patches].T,
+        gti[0:ks, patches].reshape(1, ks),
+        tbo[6, 0:patches],
+        gwi,
+        vec[5, 0:shard],
+        gwo.T,
+        vec[4, 0:shard],
+        sm[n_dp : n_dp + count, 0],
+        sm[0:n_dp, 0 : count - QRY_DEV],
+    )
 
 
 def layer_norm(values, gain, shift):
@@ -120,23 +999,20 @@
     chan_cube = chan_in.reshape(count, patches, width)
     pre_cube = d_pre.reshape(count, patches, -1)
     hidden_cube = hidden.reshape(count, patches, -1)
-    own_in = jnp.einsum("nsd,nsh->ndh", chan_cube, pre_cube, preferred_element_type=jnp.float32)
-    own_out = jnp.einsum("nsd,nsh->ndh", cotangent, hidden_cube, preferred_element_type=jnp.float32)
-    squares = jnp.sum(own_in * own_in, axis=(1, 2)) + jnp.sum(own_out * own_out, axis=(1, 2))
-    train_in = own_in[QRY_DEV:]
-    train_out = own_out[QRY_DEV:]
-    query_chan = lax.all_gather(chan_cube[:QRY_DEV], "dp", axis=0, tiled=True)
-    query_pre = lax.all_gather(pre_cube[:QRY_DEV], "dp", axis=0, tiled=True)
-    query_hidden = lax.all_gather(hidden_cube[:QRY_DEV], "dp", axis=0, tiled=True)
-    query_dout = lax.all_gather(cotangent[:QRY_DEV], "dp", axis=0, tiled=True)
-    query_in = jnp.einsum("qsd,qsh->qdh", query_chan, query_pre, preferred_element_type=jnp.float32)
-    query_out = jnp.einsum(
-        "qsd,qsh->qdh", query_dout, query_hidden, preferred_element_type=jnp.float32
-    )
-    values = jnp.einsum("qab,tab->qt", query_in, train_in, precision=HIGH) + jnp.einsum(
-        "qab,tab->qt", query_out, train_out, precision=HIGH
-    )
-    influence = values
+    def against(chan, pre, dout, low):
+        grams = [
+            jnp.einsum("sd,npd->nsp", a, b, preferred_element_type=jnp.float32)
+            for a, b in ((chan, chan_cube), (pre, pre_cube), (dout, cotangent), (low, hidden_cube))
+        ]
+        return jnp.sum(grams[0] * grams[1] + grams[2] * grams[3], axis=(1, 2))
+
+    own = lax.map(lambda a: against(*a), (chan_cube, pre_cube, cotangent, hidden_cube))
+    squares = jnp.diagonal(own)
+    queries = tuple(
+        lax.all_gather(a[:QRY_DEV], "dp", axis=0, tiled=True)
+        for a in (chan_cube, pre_cube, cotangent, hidden_cube)
+    )
+    influence = lax.map(lambda a: against(*a), queries)[:, QRY_DEV:]
     influence, squares = lax.psum((influence, squares), "tensor")
     sqnorms = squares / (2.0 * D * FF)
     influence = influence * (2.0 * D * FF) ** (-0.5)
@@ -173,8 +1049,11 @@
         P("tensor", None),
         P(),
     )
+    n_dp = mesh.shape["dp"]
+    fits = n_dp % 2 == 0 and n_dp <= 8 and mesh.shape["tensor"] == 4
+    device = functools.partial(fused, n_dp) if fits else per_device
     return jax.shard_map(
-        per_device,
+        device,
         mesh=mesh,
         in_specs=placed,
         out_specs=(

time: 660 us -> 103 us (0.16); the launches traced: 651 us -> 103 us
  waiting for transfers between devices: 325 us -> 0 us
  matrix products: 143 us -> 0 us
  Pallas kernels: 0 us -> 81.2 us
  blocking collectives: 76 us -> 0 us
  local copies, waits for them, and re-layouts: 69.3 us -> 20.8 us
  other arithmetic: 20.2 us -> 0 us
  between operations: 16.3 us -> 0.67 us
    dot_general x18 -> x0, matrix products: 143 us -> none  [the longest x1 44.7 us: per_device(): jnp.einsum('qab,tab->qt', query_in, train_in, precision=HIGH)]
    psum x1 -> x0, waiting for transfers between devices: 137 us -> none  [per_device(): mixed = lax.psum(partial_out, 'tensor')]
    all_gather x4 -> x0, waiting for transfers between devices: 89.5 us -> none  [the longest x1 31.5 us: per_device(): query_pre = lax.all_gather(pre_cube[:QRY_DEV], 'dp', axis=0, tiled=True)]
    pallas_call x0 -> x1, Pallas kernels: none -> 81.2 us  [fused(): pl.pallas_call(body, out_shape=[jax.ShapeDtypeStruct(s, d) for s, d, _ in...]
    reduce_scatter x3 -> x0, waiting for transfers between devices: 75.4 us -> none  [the longest x1 37.8 us: per_device(): lax.psum_scatter(grad_first, 'dp', scatter_dimension=1, tiled=True)]
    all_gather x4 -> x0, blocking collectives: 36.4 us -> none  [the longest x1 10.9 us: per_device(): lax.all_gather(tok_out_t, 'dp', axis=1, tiled=True)]
    psum x2 -> x0, blocking collectives: 26.4 us -> none  [the longest x1 14.7 us: per_device(): total_tbias_out = lax.psum(grad_tbias_out, 'dp')]
    unnamed x16 -> x0, waiting for transfers between devices: 22.5 us -> none
  transfers between devices with their start and end apart: 12 -> 0, of which waited for: 8 -> 0; matrix products, arithmetic and copies ran while one was open for 29% -> 0% of each run, Pallas kernels for 0% -> 0%
where the time goes in v1:
time: 103 us
  Pallas kernels  81.2 us (79%)
  local copies, waits for them, and re-layouts  20.8 us (20%)
    pallas_call x1, Pallas kernels, fused(): pl.pallas_call(body, out_shape=[jax.ShapeDtypeStruct(s, d) for s, d, _ in...  81.2 us
    unnamed x13, local copies, waits for them, and re-layouts  8.28 us

profile of v1, /device:TPU:0, one launch (start us, length us, event | category | flops | bytes accessed | tf_op | source)
XLA Modules:
  0.0 102.7 jit_solution(15385211862063895294)
XLA Ops:
  0.6 1.5 %copy.29.refs_6_ = bf16[196,48]{1,0:T(8,128)(2,1)} copy(bf16[196,48]{0,1:T(8,128)(2,1)} %param.16) | data formatting | bytes 37632 | tf_op args[4]
  2.1 1.5 %copy.30.refs_7_ = bf16[196,48]{1,0:T(8,128)(2,1)} copy(bf16[196,48]{0,1:T(8,128)(2,1)} %param.17) | data formatting | bytes 37632 | tf_op args[5]
  3.6 1.3 %reshape.47.refs_10_ = f32[1,768]{1,0:T(1,128)} reshape(bf16[768]{0:T(1024)(128)(2,1)} %param.21) | data formatting | bytes 4608 | tf_op jit(solution)/shard_map/reshape | solution.py:872
  4.8 1.3 %reshape.49.refs_11_ = f32[1,768]{1,0:T(1,128)} reshape(bf16[768]{0:T(1024)(128)(2,1)} %param.23) | data formatting | bytes 4608 | tf_op jit(solution)/shard_map/reshape | solution.py:873
  6.1 1.2 %reshape.41.refs_9_ = bf16[1,196]{1,0:T(2,128)(2,1)} reshape(bf16[196]{0:T(256)(128)(2,1)} %param.19) | data formatting | bytes 784 | tf_op jit(solution)/shard_map/reshape | solution.py:871
  7.3 81.2 %mixer.1 = (bf16[3,196,768]{2,1,0:T(8,128)(2,1)}, bf16[3,196,768]{2,1,0:T(8,128)(2,1)}, f32[96,768]{1,0:T(8,128)}, f32[96,768]{1,0:T(8,128)}, f32[48,256]{1,0:T(...) custom-call(bf16[3,196,768]{2,1,0:T(8,128)(2,1)} %refs_0_.1, ...), custom_call_target="tpu_custom_call" | custom-call | tf_op jit(solution)/shard_map/mixer/pallas_call | solution.py:851
  88.5 0.0 copy-start
  88.5 1.5 %slice_bitcast_fusion = (f32[196,48]{0,1:T(8,128)}, f32[196,48]{0,1:T(8,128)}) fusion(f32[48,256]{1,0:T(8,128)} %get-tuple-element.27, f32[48,256]{1,0:T(8,128)} %get-tuple-element.26), kind=kLoop, calls=%fused_computation | loop fusion | bytes 150528 | tf_op jit(solution)/shard_map/transpose | solution.py:881
  90.0 1.3 %fusion = (f32[2,96]{1,0:T(2,128)}, f32[2,96]{1,0:T(2,128)}) fusion(f32[8,128]{1,0:T(8,128)} %get-tuple-element.25), kind=kLoop, calls=%fused_computation.6 | loop fusion | bytes 3072 | tf_op jit(solution)/shard_map/slice | solution.py:879
  91.4 1.3 %slice_bitcast_fusion.2 = (f32[96]{0:T(128)}, f32[96]{0:T(128)}) fusion(f32[8,128]{1,0:T(8,128)} %get-tuple-element.25), kind=kLoop, calls=%fused_computation.4 | loop fusion | bytes 1536 | tf_op jit(solution)/shard_map/squeeze | solution.py:887
  92.6 0.7 slice.39
  93.3 0.6 copy.31
  93.9 1.4 %slice_reduce_fusion = f32[48]{0:T(128)} fusion(f32[48,256]{1,0:T(8,128)} %get-tuple-element.26), kind=kLoop, calls=%fused_computation.2 | loop fusion | bytes 384 | tf_op jit(solution)/shard_map/slice | solution.py:882
  95.4 1.3 %slice_reduce_fusion.1 = f32[3]{0:T(128)} fusion(f32[16,128]{1,0:T(8,128)} %get-tuple-element.31), kind=kLoop, calls=%fused_computation.3 | loop fusion | bytes 24 | tf_op jit(solution)/shard_map/slice | solution.py:888
  96.7 1.3 %slice.35 = f32[1,196]{1,0:T(1,128)} slice(f32[8,256]{1,0:T(8,128)} %get-tuple-element.28), slice={[6:7], [0:196]} | slice | bytes 1568 | tf_op jit(solution)/shard_map/slice | solution.py:883
  97.9 2.2 %copy.36 = bf16[3,196,768]{2,1,0:T(8,128)(2,1)} copy(bf16[3,196,768]{2,1,0:T(8,128)(2,1)} %get-tuple-element.80) | data formatting | bytes 1806336
  100.1 0.0 copy-done
  100.1 0.0 copy-start.2
  100.1 0.0 copy-start.1
  100.1 0.9 copy.37
  101.0 0.2 copy-done.2
  101.2 0.7 copy.38
  102.0 0.0 copy-done.1
  102.0 0.7 copy.39
Async XLA Ops:
  88.5 11.6 %copy-start = (bf16[3,196,768]{2,1,0:T(8,128)(2,1)S(1)}, bf16[3,196,768]{2,1,0:T(8,128)(2,1)}, u32[]{:S(2)}) copy-start(bf16[3,196,768]{2,1,0:T(8,128)(2,1)} %get-tuple-element.81) | copy-start | bytes 2709508
  100.1 1.1 %copy-start.2 = (f32[96,768]{1,0:T(8,128)S(1)}, f32[96,768]{1,0:T(8,128)}, u32[]{:S(2)}) copy-start(f32[96,768]{1,0:T(8,128)} %get-tuple-element.88) | copy-start | bytes 884740
  100.1 1.8 %copy-start.1 = (f32[96,768]{1,0:T(8,128)S(1)}, f32[96,768]{1,0:T(8,128)}, u32[]{:S(2)}) copy-start(f32[96,768]{1,0:T(8,128)} %get-tuple-element.30) | copy-start | bytes 884740

commit v2 on v1

--- a/solution.py
+++ b/solution.py
@@ -90,6 +90,7 @@
     toki,
     toko,
     gs,
+    bs,
     dout,
     dhid,
     xf,
@@ -173,13 +174,10 @@
     tail = patches - last
 
     def peer(k):
-        return ((chip + k) % nc) * 2 + core
-
-    def src(k):
-        return ((chip - k + nc) % nc) * 2 + core
-
-    def src_sib(k):
-        return ((chip - k + nc) % nc) * 2 + 1 - core
+        return (chip ^ k) * 2 + core
+
+    def peer_sib(k):
+        return (chip ^ k) * 2 + 1 - core
 
     def rcopy(a, b, ss, rs, dev):
         return pltpu.make_async_remote_copy(
@@ -190,37 +188,37 @@
         def __init__(self, buf, c, x):
             self.buf, self.c, self.x = buf, c, x
 
-        def chip_copy(self, k):
-            return rcopy(
-                self.buf.at[me], self.buf.at[me], self.c.at[0, k - 1], self.c.at[1, k - 1], (peer(k), t)
-            )
+        def chip_copy(self, block, k, n):
+            b = self.buf.at[block]
+            return rcopy(b, b, self.c.at[0, n], self.c.at[1, n], (peer(k), t))
 
         def sib_copy(self, k):
-            s = src(k)
-            return rcopy(self.buf.at[s], self.buf.at[s], self.x.at[0, k], self.x.at[1, k], (sib, t))
-
-        def start(self):
-            for k in range(1, nc):
-                self.chip_copy(k).start()
+            b = self.buf.at[peer(k)]
+            return rcopy(b, b, self.x.at[0, k], self.x.at[1, k], (sib, t))
+
+        def start(self, across=False):
+            for k in (1, 2, 3) if across else (1, 2):
+                self.chip_copy(me, k, k - 1).start()
             self.sib_copy(0).start()
 
-        def relay(self, k):
-            s = src(k)
-            rcopy(
-                self.buf.at[s], self.buf.at[s], self.c.at[0, k - 1], self.c.at[1, k - 1], (sib, t)
-            ).wait_recv()
+        def relay(self, k, across=False):
+            self.chip_copy(peer(k), k, k - 1).wait_recv()
+            if k < 3 and not across:
+
+                @pl.when(core == k - 1)
+                def _():
+                    self.chip_copy(peer(k), 3 - k, 2).start()
+
             self.sib_copy(k).start()
 
         def from_sib(self, k):
-            s = src_sib(k)
-            rcopy(
-                self.buf.at[s], self.buf.at[s], self.x.at[0, k], self.x.at[1, k], (sib, t)
-            ).wait_recv()
+            b = self.buf.at[peer_sib(k)]
+            rcopy(b, b, self.x.at[0, k], self.x.at[1, k], (sib, t)).wait_recv()
 
         def drain(self):
-            for k in range(1, nc):
-                self.chip_copy(k).wait_send()
-            for k in range(nc):
+            for n in range(3):
+                self.chip_copy(me, n + 1, n).wait_send()
+            for k in range(4):
                 self.sib_copy(k).wait_send()
 
     params = Gather(pb, pb_c, pb_x)
@@ -246,19 +244,17 @@
         lax.broadcasted_iota(jnp.int32, (kb, 128), 0) == lax.broadcasted_iota(jnp.int32, (kb, 128), 1)
     ).astype(BF16)
     aug[...] = jnp.zeros(aug.shape, F32)
-    aug[0:patches, 0:ks] = tok_in_r[...].astype(F32)
     aug[patches : patches + 1, 0:ks] = tok_bias_r[...].astype(F32)
     pb[me, 0:kb, 0:ROWS] = dot_nt(eye, aug[...].astype(BF16)).astype(BF16)
-    aug[0:patches, 0:ks] = tok_out_r[...].astype(F32)
-    aug[patches : patches + 1, 0:ks] = jnp.zeros((1, ks), F32)
-    pb[me, kb : 2 * kb, 0:ROWS] = dot_nt(eye, aug[...].astype(BF16)).astype(BF16)
+    pb[me, 0:ks, 0:patches] = tok_in_r[...]
+    pb[me, kb : kb + ks, 0:patches] = tok_out_r[...]
     misc[...] = jnp.zeros(misc.shape, F32)
     misc[0:2, 0:shard] = gains_r[...].astype(F32)
     misc[2:4, 0:shard] = shifts_r[...].astype(F32)
     pb[me, 2 * kb : 2 * kb + 16, :] = misc[...].astype(BF16)
 
     pl.semaphore_wait(barrier, len(others))
-    params.start()
+    params.start(across=True)
 
     loads[0].wait()
     misc[...] = jnp.zeros(misc.shape, F32)
@@ -308,8 +304,8 @@
 
     lax.fori_loop(0, count, first_norm, 0)
 
-    for k in range(1, nc):
-        params.relay(k)
+    for k in (1, 2, 3):
+        params.relay(k, across=True)
     for k in range(nc):
         params.from_sib(k)
     full = jnp.zeros((16, D), F32)
@@ -321,7 +317,9 @@
         full = full + (pltpu.roll(part, d * shard, 1) if d else part)
     gs[...] = full
     misc[...] = jnp.zeros(misc.shape, F32)
-    misc[0:1, 0:patches] = tok_bias_out_r[...].astype(F32)
+    misc[0:1, 0:patches] = tok_bias_out_r[...].astype(F32).reshape(1, patches)
+    bs[0:1, :] = bias_in_r[...].astype(F32).reshape(1, D)
+    bs[1:2, :] = bias_out_r[...].astype(F32).reshape(1, D)
     toko_t[K:KA, :] = misc[...].astype(BF16)
     ri = lax.broadcasted_iota(jnp.int32, (ROWS, ROWS), 0)
     ci = lax.broadcasted_iota(jnp.int32, (ROWS, ROWS), 1)
@@ -365,16 +363,15 @@
         ztot[r, :] = (zpair[r, :].astype(F32) + zrxp[r, :].astype(F32)).astype(BF16)
         down_copy(c).start()
 
-    def zslot(s):
+    def zslot(s, pair=True, total=True):
+        if isinstance(s, int):
+            pair, total = s < steps, 0 <= s - LAG < steps
+
         @pl.when(mid)
         def _():
-            if isinstance(s, int):
-                if s < steps:
-                    zpair_step(s)
-                if 0 <= s - LAG < steps:
-                    ztot_step(s - LAG)
-            else:
+            if pair:
                 zpair_step(s)
+            if total:
                 ztot_step(s - LAG)
 
     def zfin(first, number):
@@ -421,7 +418,7 @@
             a = jnp.zeros((8, 256), F32)
             for b in range(nblk):
                 rb = pl.ds(base + 16 * b, 16)
-                value, slope = gelu_pair(tmp[16 * b : 16 * b + 16, :] + bias_in_r[:, c : c + 256])
+                value, slope = gelu_pair(tmp[16 * b : 16 * b + 16, :] + bs[0:1, c : c + 256])
                 hid[rb, c : c + 256] = value.astype(BF16)
                 low = (slope * dhid[rb, c : c + 256]).astype(BF16)
                 dpre[rb, c : c + 256] = low
@@ -430,6 +427,11 @@
         for c in range(0, D, 256):
             zpart[r, c : c + 256] = dot_nt(dpre[r, :], w_in[c : c + 256, :]).astype(BF16)
         start_up(4 * i, half - 4 * count, i == count - 1)
+
+        @pl.when(i > 0)
+        def _():
+            zslot(i - 1, total=False)
+
         return carry
 
     lax.fori_loop(0, count, forward, 0)
@@ -443,8 +445,7 @@
         return carry
 
     lax.fori_loop(0, count, partial_out, 0)
-    zslot(0)
-    zslot(1)
+    zslot(2)
 
     def weight_grad(j, carry):
         cols = pl.ds(pl.multiple_of(j * 256, 256), 256)
@@ -459,7 +460,7 @@
             wsib_s[c, m] = gw[m, rows, :].astype(BF16)
     w_sib = rcopy(wsib_s, wsib_r, w_sem.at[0, 0], w_sem.at[1, 0], (sib, t))
     w_sib.start()
-    zslot(2)
+    zslot(3)
 
     sqs[...] = jnp.zeros(sqs.shape, F32)
 
@@ -471,49 +472,41 @@
         return carry
 
     lax.fori_loop(0, count, square, 0)
-    zslot(3)
+    zslot(4)
 
     w_sib.wait_recv()
 
-    def w_chip(k):
-        return rcopy(
-            wch_s.at[k - 1], wch_r.at[k - 1], w_sem.at[0, k], w_sem.at[1, k], (peer(k), t)
-        )
-
-    for k in range(1, nc):
-        dest = (chip + k) % nc
+    def w_chip(n, k):
+        return rcopy(wch_s.at[n], wch_r.at[n], w_sem.at[0, n + 1], w_sem.at[1, n + 1], (peer(k), t))
+
+    def w_share(dest, m):
         rows = pl.ds(pl.multiple_of((2 * dest + core) * shard, 8), shard)
+        return gw[m, rows, :] + wsib_r[dest, m].astype(F32)
+
+    first, second = 1 + core, 2 - core
+    for n, dest in ((0, chip ^ 3), (1, chip ^ first)):
         for m in range(2):
-            wch_s[k - 1, m] = (gw[m, rows, :] + wsib_r[dest, m].astype(F32)).astype(BF16)
-        w_chip(k).start()
-    zslot(4)
+            wch_s[n, m] = w_share(dest, m).astype(BF16)
+        w_chip(n, first).start()
 
     infl[...] = jnp.zeros(infl.shape, F32)
 
     def query(j, carry):
         k = j // 2
         own = j % 2 == 0
-        slot = jnp.where(own, src(k), src_sib(k))
-
-        @pl.when(own & (k > 0))
-        def _():
-            dqs.relay(k)
-            cqs.relay(k)
+        slot = jnp.where(own, peer(k), peer_sib(k))
 
         @pl.when(jnp.logical_not(own))
         def _():
             dqs.from_sib(k)
             cqs.from_sib(k)
 
-        @pl.when(j + 5 < half)
-        def _():
-            zslot(j + 5)
-
+        zslot(j + jnp.where(j < 2, 5, half + LAG + 2))
         for c in range(0, D, 256):
             tmp[0:ROWS, :] = dot_nn(cq[slot], w_in[:, c : c + 256])
             tmp[ROWS : 2 * ROWS, :] = dot_nt(dq[slot], w_out[c : c + 256, :])
             for b in range(0, ROWS, 16):
-                value, slope = gelu_pair(tmp[b : b + 16, :] + bias_in_r[:, c : c + 256])
+                value, slope = gelu_pair(tmp[b : b + 16, :] + bs[0:1, c : c + 256])
                 hq[b : b + 16, c : c + 256] = value.astype(BF16)
                 pq[b : b + 16, c : c + 256] = (slope * tmp[ROWS + b : ROWS + b + 16, :]).astype(BF16)
         for q in range(count - QRY_DEV):
@@ -523,26 +516,21 @@
             infl[q, pl.ds(slot, 1), 0:ROWS] = jnp.sum(g1 + g2, axis=0, keepdims=True)
         return carry
 
-    lax.fori_loop(0, n_dp, query, 0)
-    for s in range(min(n_dp + 5, half), half + LAG):
+    lax.fori_loop(0, 2, query, 0)
+    for s in range(7, half + LAG):
         zslot(s)
-
-    lane = lax.broadcasted_iota(jnp.int32, (n_dp, 128), 1)
-    sm = jnp.zeros((n_dp, 128), F32)
-    for q in range(count - QRY_DEV):
-        sm = jnp.where(lane == q, jnp.sum(infl[q], axis=1, keepdims=True), sm)
-    zsm[t, 0:n_dp, :] = sm * (2.0 * D * FF) ** (-0.5)
-    zsm[t, n_dp : n_dp + 8, :] = jnp.broadcast_to(
-        jnp.sum(sqs[...], axis=1, keepdims=True) / (2.0 * D * FF), (8, 128)
-    )
-
-    def sm_copy(k):
-        return rcopy(
-            zsm.at[t], zsm.at[t], s_sem.at[0, k - 1], s_sem.at[1, k - 1], (me, (t + k) % 4)
-        )
-
-    for k in (1, 2, 3):
-        sm_copy(k).start()
+        if s == 7:
+            for k in (1, 2):
+                dqs.relay(k)
+        if s == 9:
+            dqs.relay(3)
+            for k in (1, 2):
+                cqs.relay(k)
+        if s == 11:
+            w_chip(0, first).wait_recv()
+            for m in range(2):
+                wch_s[2, m] = (w_share(chip ^ second, m) + wch_r[0, m].astype(F32)).astype(BF16)
+            w_chip(2, second).start()
 
     gtok[...] = jnp.zeros(gtok.shape, F32)
 
@@ -604,7 +592,6 @@
         return carry
 
     lax.fori_loop(0, count, backward, 0)
-    done = half + LAG + count
 
     for c in range(nc):
         rows = pl.ds(pl.multiple_of((2 * c + 1 - core) * kb, 8), kb)
@@ -618,7 +605,7 @@
     vec[6:7, 0:256] = gtok[1, K : K + 1, :]
     v_sib = rcopy(vec, vsib_r, v_sem.at[0, 0], v_sem.at[1, 0], (sib, t))
     v_sib.start()
-    zslot(done)
+    zslot(half + LAG + count)
     v_sib.wait_recv()
 
     def v_chip(k):
@@ -637,22 +624,43 @@
         )
 
     for k in range(1, nc):
-        dest = (chip + k) % nc
+        dest = chip ^ k
         rows = pl.ds(pl.multiple_of((2 * dest + core) * kb, 8), kb)
         for m in range(2):
             tch_s[k - 1, m] = gtok[m, rows, :] + tsib_r[dest, m]
         t_chip(k).start()
-    zslot(done + 1)
-
-    rows = pl.ds(pl.multiple_of(me * shard, 8), shard)
+
+
+    cqs.relay(3)
+    lax.fori_loop(2, n_dp, query, 0)
+    at = half + LAG + 2 + n_dp
+
+    def as_row(values):
+        totals = jnp.sum(values, axis=1, keepdims=True)
+        at = lax.broadcasted_iota(jnp.int32, (values.shape[0], 128), 0)
+        lane = lax.broadcasted_iota(jnp.int32, (values.shape[0], 128), 1)
+        return jnp.sum(jnp.where(at == lane, totals, 0.0), axis=0, keepdims=True)
+
+    zsm[t] = jnp.zeros((8, 128), F32)
+    zsm[t, 0:1, :] = as_row(sqs[...]) / (2.0 * D * FF)
+    for q in range(count - QRY_DEV):
+        zsm[t, 1 + q : 2 + q, :] = as_row(infl[q]) * (2.0 * D * FF) ** (-0.5)
+
+    def sm_copy(k):
+        return rcopy(
+            zsm.at[t], zsm.at[t], s_sem.at[0, k - 1], s_sem.at[1, k - 1], (me, (t + k) % 4)
+        )
+
+    for k in (1, 2, 3):
+        sm_copy(k).start()
+
     for m, out in enumerate((gwi_o, gwo_o)):
-        out[...] = gw[m, rows, :] + wsib_r[chip, m].astype(F32)
-    for k in range(1, nc):
-        w_chip(k).wait_recv()
+        out[...] = w_share(chip, m)
+    for n in (1, 2):
+        w_chip(n, first).wait_recv()
         for m, out in enumerate((gwi_o, gwo_o)):
-            out[...] += wch_r[k - 1, m].astype(F32)
-    zslot(done + 2)
-    zslot(done + 3)
+            out[...] += wch_r[n, m].astype(F32)
+    zslot(at)
     for k in (1, 2, 3):
         sm_copy(k).wait_recv()
     sm_o[...] = (zsm[0] + zsm[1]) + (zsm[2] + zsm[3])
@@ -671,10 +679,11 @@
     tbo_o[...] = total[:, 0:256]
     vec_o[...] = pltpu.roll(total, (D - me * shard) % D, 1)[:, 0:128]
 
+
     def act_copy(i):
         return pltpu.make_async_copy(act_s.at[i], act_o.at[i], out_sem.at[1, i])
 
-    at = done + 4
+    at += 1
     for i in range(count):
         need = -(-((i + 1) * ROWS) // CHUNK) + half
         while at < min(need + LAG, steps + LAG):
@@ -686,7 +695,7 @@
             n = min(16, patches - 16 * b)
             rb = slice(i * ROWS + 16 * b, i * ROWS + 16 * b + 16)
             ro = slice(R + i * ROWS + 16 * b, R + i * ROWS + 16 * b + 16)
-            a = (xf[rb, :] + ztot[ro, :].astype(F32) + bias_out_r[...]).astype(BF16)
+            a = (xf[rb, :] + ztot[ro, :].astype(F32) + bs[1:2, :]).astype(BF16)
             act_s[i, 16 * b : 16 * b + n, :] = a[0:n]
         act_copy(i).start()
 
@@ -715,7 +724,7 @@
     t_sib.wait_send()
     v_sib.wait_send()
     for k in range(1, nc):
-        w_chip(k).wait_send()
+        w_chip(k - 1, first).wait_send()
         t_chip(k).wait_send()
         v_chip(k).wait_send()
     for k in (1, 2, 3):
@@ -723,6 +732,40 @@
     for i in range(count):
         ing_copy(i).wait()
         act_copy(i).wait()
+
+
+def finish(shard, ks, patches, count, queries, act, ing, gwi, gwo, gti, gto, vec, tbo, sm, *refs):
+    big, small, held, sem = refs[:4], refs[4:14], refs[14:18], refs[18]
+    pieces = [(n, i) for n in (0, 1) for i in range(count)] + [(2, None), (3, None)]
+
+    def part(ref, i):
+        return ref if i is None else ref.at[i]
+
+    loads, stores = [], []
+    for at, (n, i) in enumerate(pieces):
+        kept = part(held[n], i)
+        loads.append(pltpu.make_async_copy(part((act, ing, gwi, gwo)[n], i), kept, sem.at[0, at]))
+        stores.append(pltpu.make_async_copy(kept, part(big[n], i), sem.at[1, at]))
+        loads[-1].start()
+    gains, shifts, gti_o, gto_o, gtb_o, tbo_o, gbi_o, gbo_o, sq_o, infl_o = small
+    gains[...] = vec[0:2, 0:shard]
+    shifts[...] = vec[2:4, 0:shard]
+    gbo_o[...] = vec[4:5, 0:shard]
+    gbi_o[...] = vec[5:6, 0:shard]
+    gti_o[...] = gti[0:ks, 0:patches]
+    gto_o[...] = gto[0:ks, 0:patches]
+    tbo_o[...] = tbo[6:7, 0:patches]
+    column = gti[0:ks, patches : patches + 1]
+    eye = lax.broadcasted_iota(jnp.int32, (ks, ks), 0) == lax.broadcasted_iota(jnp.int32, (ks, ks), 1)
+    gtb_o[...] = jnp.sum(jnp.where(eye, column, 0.0), axis=0, keepdims=True)
+    sq_o[...] = sm[0:1, 0:count]
+    for t in range(infl_o.shape[0]):
+        infl_o[t : t + 1, :] = sm[1 + t : 2 + t, 0:queries]
+    for load, store in zip(loads, stores):
+        load.wait()
+        store.start()
+    for store in stores:
+        store.wait()
 
 
 def fused(
@@ -756,7 +799,6 @@
     vm = pl.BlockSpec(memory_space=pltpu.VMEM)
     V = pltpu.VMEM
     dma = lambda *s: pltpu.SemaphoreType.DMA(s)
-    smr = n_dp + 8
     scratch = dict(
         x_raw=V((count, patches, D), BF16),
         d_raw=V((count, patches, D), BF16),
@@ -772,6 +814,7 @@
         toki=V((ROWS, KL), BF16),
         toko=V((ROWS, KL), BF16),
         gs=V((16, D), F32),
+        bs=V((8, D), F32),
         dout=V((R, D), BF16),
         dhid=V((R, hidden), F32),
         xf=V((R, D), F32),
@@ -814,7 +857,7 @@
         vec=V((8, D), F32),
         vsib_r=V((8, D), F32),
         vch=V((nc, 8, D), F32),
-        zsm=V((4, smr, 128), F32),
+        zsm=V((4, 8, 128), F32),
         in_sem=dma(4),
         out_sem=dma(2, count),
         pb_c=dma(2, nc - 1),
@@ -840,7 +883,7 @@
         ((kb, 256), F32, vm),
         ((8, 128), F32, vm),
         ((8, 256), F32, vm),
-        ((smr, 128), F32, vm),
+        ((8, 128), F32, vm),
     ]
     names = list(scratch)
     n_in, n_out = 12, len(outs)
@@ -865,28 +908,62 @@
         w_out,
         norm_gains,
         norm_shifts,
-        tok_in,
-        tok_out_t,
+        tok_in.T,
+        tok_out_t.T,
         tok_bias_in,
-        tok_bias_out.reshape(1, -1),
-        bias_in.astype(F32).reshape(1, -1),
-        bias_out.astype(F32).reshape(1, -1),
-    )
+        tok_bias_out,
+        bias_in,
+        bias_out,
+    )
+    queries, trains = n_dp * QRY_DEV, count - QRY_DEV
+    out = pl.pallas_call(
+        functools.partial(finish, shard, ks, patches, count, queries),
+        out_shape=[
+            jax.ShapeDtypeStruct(s, d)
+            for s, d in (
+                (images.shape, BF16),
+                (images.shape, BF16),
+                ((shard, hidden), F32),
+                ((shard, hidden), F32),
+                ((2, shard), F32),
+                ((2, shard), F32),
+                ((ks, patches), F32),
+                ((ks, patches), F32),
+                ((1, ks), F32),
+                ((1, patches), F32),
+                ((1, shard), F32),
+                ((1, shard), F32),
+                ((1, count), F32),
+                ((trains, queries), F32),
+            )
+        ],
+        in_specs=[anyspace] * 4 + [vm] * 5,
+        out_specs=[anyspace] * 4 + [vm] * 10,
+        scratch_shapes=[
+            V(images.shape, BF16),
+            V(images.shape, BF16),
+            V((shard, hidden), F32),
+            V((shard, hidden), F32),
+            dma(2, 2 * count + 2),
+        ],
+        name="finish",
+    )(act, ing, gwi, gwo, gti, gto, vec, tbo, sm)
+    act, ing, gwi, gwo, gains, shifts, gti, gto, gtb, tbo, gbi, gbo, squares, influence = out
     return (
         act,
         ing,
-        vec[0:2, 0:shard],
-        vec[2:4, 0:shard],
-        gti[0:ks, 0:patches].T,
-        gto[0:ks, 0:patches].T,
-        gti[0:ks, patches].reshape(1, ks),
-        tbo[6, 0:patches],
+        gains,
+        shifts,
+        gti.T,
+        gto.T,
+        gtb,
+        tbo.reshape(patches),
         gwi,
-        vec[5, 0:shard],
+        gbi.reshape(shard),
         gwo.T,
-        vec[4, 0:shard],
-        sm[n_dp : n_dp + count, 0],
-        sm[0:n_dp, 0 : count - QRY_DEV],
+        gbo.reshape(shard),
+        squares.reshape(count),
+        influence.T,
     )
 
 
@@ -1050,7 +1127,7 @@
         P(),
     )
     n_dp = mesh.shape["dp"]
-    fits = n_dp % 2 == 0 and n_dp <= 8 and mesh.shape["tensor"] == 4
+    fits = n_dp == 8 and mesh.shape["tensor"] == 4
     device = functools.partial(fused, n_dp) if fits else per_device
     return jax.shard_map(
         device,

time: 103 us -> 81.9 us (0.80)
  local copies, waits for them, and re-layouts: 20.8 us -> 0 us
    unnamed x13 -> x0, local copies, waits for them, and re-layouts: 8.28 us -> none
    slice x5 -> x0, local copies, waits for them, and re-layouts: 5.99 us -> none  [the longest x1 1.43 us: fused(): gti[0:ks, patches].reshape(1, ks)]
    pallas_call x1, Pallas kernels: 81.2 us -> 76.9 us  [fused(): pl.pallas_call(body, out_shape=[jax.ShapeDtypeStruct(s, d) for s, d, _ in...]
    pallas_call x0 -> x1, Pallas kernels: none -> 4.05 us  [fused(): pl.pallas_call(functools.partial(finish, shard, ks, patches, count, queri...]
    reshape x3 -> x0, local copies, waits for them, and re-layouts: 3.74 us -> none  [the longest x1 1.26 us: fused(): bias_out.astype(F32).reshape(1, -1)]
    transpose x1 -> x0, local copies, waits for them, and re-layouts: 1.54 us -> none  [fused(): gto[0:ks, 0:patches]]
    squeeze x1 -> x0, local copies, waits for them, and re-layouts: 1.27 us -> none  [fused(): vec[4, 0:shard]]
where the time goes in v2:
time: 81.9 us; the launch traced here: 81.6 us
  Pallas kernels  81 us (99%)
    pallas_call x1, Pallas kernels, fused(): pl.pallas_call(body, out_shape=[jax.ShapeDtypeStruct(s, d) for s, d, _ in...  76.9 us
    pallas_call x1, Pallas kernels, fused(): pl.pallas_call(functools.partial(finish, shard, ks, patches, count, queri...  4.05 us

profile of v2, /device:TPU:0, one launch (start us, length us, event | category | flops | bytes accessed | tf_op | source)
XLA Modules:
  0.0 81.6 jit_solution(12072152903533510371)
XLA Ops:
  0.6 76.9 %mixer.1 = (bf16[3,196,768]{2,1,0:T(8,128)(2,1)}, bf16[3,196,768]{2,1,0:T(8,128)(2,1)}, f32[96,768]{1,0:T(8,128)}, f32[96,768]{1,0:T(8,128)}, f32[48,256]{1,0:T(...) custom-call(bf16[3,196,768]{2,1,0:T(8,128)(2,1)} %refs_0_.1, ...), custom_call_target="tpu_custom_call" | custom-call | tf_op jit(solution)/shard_map/mixer/pallas_call | solution.py:894
  77.6 4.0 %finish.1 = (bf16[3,196,768]{2,1,0:T(8,128)(2,1)}, bf16[3,196,768]{2,1,0:T(8,128)(2,1)}, f32[96,768]{1,0:T(8,128)}, f32[96,768]{1,0:T(8,128)}, f32[2,96]{1,0:T(2...) custom-call(bf16[3,196,768]{2,1,0:T(8,128)(2,1)} %get-tuple-element., ...), custom_call_target="tpu_custom_call" | custom-call | tf_op jit(solution)/shard_map/finish/pallas_call | solution.py:919

commit v3 on v2

--- a/solution.py
+++ b/solution.py
@@ -16,8 +16,6 @@
 BF16 = jnp.bfloat16
 
 ROWS = 208
-CHUNK = 48
-LAG = 2
 C1 = 0.7978845608028654
 C2 = 0.044715
 
@@ -41,6 +39,11 @@
     value = v * hp
     slope = hp + (0.5 * v) * (1.0 - th * th) * (C1 + (3.0 * C1 * C2) * u)
     return value, slope
+
+
+def z_sizes(count):
+    full = [64] * (3 * count)
+    return full + [16, 16] + full
 
 
 def fold(v):
@@ -59,14 +62,14 @@
     cotangent,
     w_in_h,
     w_out_h,
-    gains_r,
-    shifts_r,
-    tok_in_r,
-    tok_out_r,
-    tok_bias_r,
-    tok_bias_out_r,
-    bias_in_r,
-    bias_out_r,
+    gains_h,
+    shifts_h,
+    tok_in_h,
+    tok_out_h,
+    tok_bias_h,
+    tok_bias_out_h,
+    bias_in_h,
+    bias_out_h,
     act_o,
     ing_o,
     gwi_o,
@@ -76,6 +79,14 @@
     vec_o,
     tbo_o,
     sm_o,
+    gains_r,
+    shifts_r,
+    tok_in_r,
+    tok_out_r,
+    tok_bias_r,
+    tok_bias_out_r,
+    bias_in_r,
+    bias_out_r,
     x_raw,
     d_raw,
     w_in,
@@ -114,6 +125,8 @@
     dmix,
     dtok,
     dnorm,
+    tails,
+    rests,
     zpart,
     zrx,
     zpair,
@@ -136,15 +149,11 @@
     zsm,
     in_sem,
     out_sem,
-    pb_c,
-    pb_x,
-    dq_c,
-    dq_x,
-    cq_c,
-    cq_x,
-    ze,
-    zm,
-    zt,
+    pb_sem,
+    dq_sem,
+    cq_sem,
+    z_sem,
+    z_sent,
     w_sem,
     t_sem,
     v_sem,
@@ -167,8 +176,6 @@
     K = n_dp * kb
     KA = K + 16
     R = count * ROWS
-    half = R // CHUNK
-    steps = 2 * half
     nblk = ROWS // 16
     last = ROWS - 16
     tail = patches - last
@@ -185,16 +192,16 @@
         )
 
     class Gather:
-        def __init__(self, buf, c, x):
-            self.buf, self.c, self.x = buf, c, x
+        def __init__(self, buf, sem):
+            self.buf, self.sem = buf, sem
 
         def chip_copy(self, block, k, n):
             b = self.buf.at[block]
-            return rcopy(b, b, self.c.at[0, n], self.c.at[1, n], (peer(k), t))
+            return rcopy(b, b, self.sem.at[0], self.sem.at[1 + n], (peer(k), t))
 
         def sib_copy(self, k):
             b = self.buf.at[peer(k)]
-            return rcopy(b, b, self.x.at[0, k], self.x.at[1, k], (sib, t))
+            return rcopy(b, b, self.sem.at[0], self.sem.at[4 + k], (sib, t))
 
         def start(self, across=False):
             for k in (1, 2, 3) if across else (1, 2):
@@ -213,42 +220,49 @@
 
         def from_sib(self, k):
             b = self.buf.at[peer_sib(k)]
-            rcopy(b, b, self.x.at[0, k], self.x.at[1, k], (sib, t)).wait_recv()
+            rcopy(b, b, self.sem.at[0], self.sem.at[4 + k], (sib, t)).wait_recv()
 
         def drain(self):
-            for n in range(3):
-                self.chip_copy(me, n + 1, n).wait_send()
-            for k in range(4):
-                self.sib_copy(k).wait_send()
-
-    params = Gather(pb, pb_c, pb_x)
-    dqs = Gather(dq, dq_c, dq_x)
-    cqs = Gather(cq, cq_c, cq_x)
-
-    loads = [
-        pltpu.make_async_copy(cotangent, d_raw, in_sem.at[0]),
-        pltpu.make_async_copy(w_out_h, w_out, in_sem.at[1]),
-        pltpu.make_async_copy(images, x_raw, in_sem.at[2]),
-        pltpu.make_async_copy(w_in_h, w_in, in_sem.at[3]),
-    ]
-    for c in loads:
-        c.start()
+            b = self.buf.at[pl.ds(0, 7)]
+            rcopy(b, b, self.sem.at[0], self.sem.at[1], (sib, t)).wait_send()
+
+    params, dqs, cqs = Gather(pb, pb_sem), Gather(dq, dq_sem), Gather(cq, cq_sem)
 
     barrier = pltpu.get_barrier_semaphore()
     others = [(sib, t)] + [(peer(k), t) for k in range(1, nc)] + [(me, (t + k) % 4) for k in (1, 2, 3)]
     for dev in others:
         pl.semaphore_signal(barrier, inc=1, device_id=dev, device_id_type=MESH)
+
+    pairs = [
+        (gains_h, gains_r),
+        (shifts_h, shifts_r),
+        (tok_in_h, tok_in_r),
+        (tok_out_h, tok_out_r),
+        (tok_bias_h, tok_bias_r),
+        (cotangent, d_raw),
+        (w_out_h, w_out),
+        (images, x_raw),
+        (w_in_h, w_in),
+        (tok_bias_out_h, tok_bias_out_r),
+        (bias_in_h, bias_in_r),
+        (bias_out_h, bias_out_r),
+    ]
+    loads = [pltpu.make_async_copy(a, b, in_sem.at[n]) for n, (a, b) in enumerate(pairs)]
+    for c in loads:
+        c.start()
 
     pb[me] = jnp.zeros(pb.shape[1:], BF16)
     eye = (
         lax.broadcasted_iota(jnp.int32, (kb, 128), 0) == lax.broadcasted_iota(jnp.int32, (kb, 128), 1)
     ).astype(BF16)
     aug[...] = jnp.zeros(aug.shape, F32)
+    misc[...] = jnp.zeros(misc.shape, F32)
+    for c in loads[:5]:
+        c.wait()
     aug[patches : patches + 1, 0:ks] = tok_bias_r[...].astype(F32)
     pb[me, 0:kb, 0:ROWS] = dot_nt(eye, aug[...].astype(BF16)).astype(BF16)
     pb[me, 0:ks, 0:patches] = tok_in_r[...]
     pb[me, kb : kb + ks, 0:patches] = tok_out_r[...]
-    misc[...] = jnp.zeros(misc.shape, F32)
     misc[0:2, 0:shard] = gains_r[...].astype(F32)
     misc[2:4, 0:shard] = shifts_r[...].astype(F32)
     pb[me, 2 * kb : 2 * kb + 16, :] = misc[...].astype(BF16)
@@ -256,12 +270,12 @@
     pl.semaphore_wait(barrier, len(others))
     params.start(across=True)
 
-    loads[0].wait()
+    loads[5].wait()
     misc[...] = jnp.zeros(misc.shape, F32)
     acc[...] = jnp.zeros(acc.shape, F32)
 
-    def pad_dout(i, carry):
-        base = pl.multiple_of(i * ROWS, 16)
+    def pad_dout(i):
+        base = i * ROWS
         dout[pl.ds(base, last), :] = d_raw[i, 0:last, :]
         for c in range(0, D, 256):
             misc[0:tail, :] = d_raw[i, last:patches, c : c + 256].astype(F32)
@@ -270,26 +284,25 @@
         for b in range(nblk):
             a = a + fold(dout[pl.ds(base + 16 * b, 16), :].astype(F32))
         acc[4] += a
-        return carry
-
-    lax.fori_loop(0, count, pad_dout, 0)
+
+    for i in range(count):
+        pad_dout(i)
     dq[me] = dout[0:ROWS, :]
-    dqs.start()
-
-    loads[1].wait()
-
-    def hidden_grad(i, carry):
-        r = pl.ds(pl.multiple_of(i * ROWS, 16), ROWS)
+
+    loads[6].wait()
+
+    def hidden_grad(i):
+        r = pl.ds(i * ROWS, ROWS)
         for c in range(0, D, 256):
             dhid[r, c : c + 256] = dot_nt(dout[r, :], w_out[c : c + 256, :])
-        return carry
-
-    lax.fori_loop(0, count, hidden_grad, 0)
-
-    loads[2].wait()
-
-    def first_norm(i, carry):
-        base = pl.multiple_of(i * ROWS, 16)
+
+    for i in range(count):
+        hidden_grad(i)
+
+    loads[7].wait()
+
+    def first_norm(i):
+        base = i * ROWS
         xf[pl.ds(base + last, 16), :] = jnp.zeros((16, D), F32)
         xf[pl.ds(base, last), :] = x_raw[i, 0:last, :].astype(F32)
         xf[pl.ds(base + last, tail), :] = x_raw[i, last:patches, :].astype(F32)
@@ -300,14 +313,17 @@
             inv = lax.rsqrt(jnp.mean(center * center, axis=-1, keepdims=True) + 1e-06)
             xh1[r, :] = center * inv
             rs1[r, :] = jnp.broadcast_to(inv, (16, 128))
-        return carry
-
-    lax.fori_loop(0, count, first_norm, 0)
+
+    for i in range(count):
+        first_norm(i)
 
     for k in (1, 2, 3):
         params.relay(k, across=True)
     for k in range(nc):
         params.from_sib(k)
+    dqs.start()
+    for c in loads[8:]:
+        c.wait()
     full = jnp.zeros((16, D), F32)
     for d in range(n_dp):
         toki_t[d * kb : (d + 1) * kb, :] = pb[d, 0:kb, :]
@@ -326,62 +342,80 @@
     eye_rows = ((ri == ci) & (ri < patches)).astype(BF16)
     toki[:, 0:K] = dot_nt(eye_rows, toki_t[:, 0:ROWS]).astype(BF16)
     toko[:, 0:KA] = dot_nt(eye_rows, toko_t[:, 0:ROWS]).astype(BF16)
-    loads[3].wait()
+
+    chunks = []
+    at = 0
+    for n in z_sizes(count):
+        chunks.append((at, n))
+        at += n
+    steps = len(chunks)
+    seam = [c for c in range(steps) if chunks[c][0] == count * last][0]
+    d_rows, o_rows = 0, count * last + 32
 
     def zrows(c):
-        return pl.ds(pl.multiple_of(c * CHUNK, 16), CHUNK)
-
-    def up_copy(c):
-        return rcopy(zpart.at[zrows(c)], zrx.at[zrows(c)], ze.at[0, c], ze.at[1, c], (me, end_peer))
-
-    def mid_copy(c):
-        return rcopy(zpair.at[zrows(c)], zrxp.at[zrows(c)], zm.at[0, c], zm.at[1, c], (me, mid_peer))
-
-    def down_copy(c):
-        return rcopy(ztot.at[zrows(c)], ztot.at[zrows(c)], zt.at[0, c], zt.at[1, c], (me, mid_end))
-
-    def start_up(first, extra, more):
+        return pl.ds(chunks[c][0], chunks[c][1])
+
+    def chunks_of(start, i):
+        return [c for c in range(steps) if start + i * last <= chunks[c][0] < start + (i + 1) * last]
+
+    def up_copy(c, r):
+        return rcopy(zpart.at[r], zrx.at[r], z_sent.at[0], z_sem.at[0, c], (me, end_peer))
+
+    def mid_copy(c, r):
+        return rcopy(zpair.at[r], zrxp.at[r], z_sent.at[1], z_sem.at[1, c], (me, mid_peer))
+
+    def down_copy(c, r):
+        return rcopy(ztot.at[r], ztot.at[r], z_sent.at[2], z_sem.at[2, c], (me, mid_end))
+
+    def start_up(some):
         @pl.when(end)
         def _():
-            for j in range(4):
-                up_copy(first + j).start()
-
-            @pl.when(more)
+            for c in some:
+                up_copy(c, zrows(c)).start()
+
+    def zpair_step(c):
+        r = zrows(c)
+        up_copy(c, r).wait_recv()
+        zpair[r, :] = (zpart[r, :].astype(F32) + zrx[r, :].astype(F32)).astype(BF16)
+        mid_copy(c, r).start()
+
+    def ztot_step(c):
+        r = zrows(c)
+        mid_copy(c, r).wait_recv()
+        ztot[r, :] = (zpair[r, :].astype(F32) + zrxp[r, :].astype(F32)).astype(BF16)
+        down_copy(c, r).start()
+
+    slots = [[c] for c in range(seam)] + [[seam, seam + 1]] + [[c] for c in range(seam + 2, steps)]
+    ticks = iter(range(len(slots) + 2))
+
+    def tick(until=None):
+        for n in ticks:
+            ups = slots[n] if n < len(slots) else []
+            downs = slots[n - 2] if n >= 2 else []
+
+            @pl.when(mid)
             def _():
-                for j in range(4, 4 + extra):
-                    up_copy(first + j).start()
-
-    def zpair_step(c):
-        up_copy(c).wait_recv()
-        r = zrows(c)
-        zpair[r, :] = (zpart[r, :].astype(F32) + zrx[r, :].astype(F32)).astype(BF16)
-        mid_copy(c).start()
-
-    def ztot_step(c):
-        mid_copy(c).wait_recv()
-        r = zrows(c)
-        ztot[r, :] = (zpair[r, :].astype(F32) + zrxp[r, :].astype(F32)).astype(BF16)
-        down_copy(c).start()
-
-    def zslot(s, pair=True, total=True):
-        if isinstance(s, int):
-            pair, total = s < steps, 0 <= s - LAG < steps
-
-        @pl.when(mid)
-        def _():
-            if pair:
-                zpair_step(s)
-            if total:
-                ztot_step(s - LAG)
-
-    def zfin(first, number):
+                for c in ups:
+                    zpair_step(c)
+                for c in downs:
+                    ztot_step(c)
+
+            if until is None or until in downs:
+                return
+
+    def zfin(some):
         @pl.when(end)
         def _():
-            for j in range(number):
-                down_copy(first + j).wait_recv()
-
-    def forward(i, carry):
-        base = pl.multiple_of(i * ROWS, 16)
+            for c in some:
+                down_copy(c, zrows(c)).wait_recv()
+
+    def pack_tails():
+        rows = [tails[i, 0:tail, :] for i in range(count)]
+        rows.append(jnp.zeros((16 - count * tail, D), F32))
+        return jnp.concatenate(rows, axis=0).astype(BF16)
+
+    def forward(i):
+        base = i * ROWS
         r = pl.ds(base, ROWS)
         for b in range(nblk):
             rb = pl.ds(base + 16 * b, 16)
@@ -408,8 +442,7 @@
             rs2[rb, :] = jnp.broadcast_to(inv, (16, 128))
             chan[rb, :] = (xhat * gs[1:2, :] + gs[3:4, :]).astype(BF16)
 
-        @pl.when(i == 0)
-        def _():
+        if i == 0:
             cq[me] = chan[0:ROWS, :]
             cqs.start()
 
@@ -425,54 +458,59 @@
                 a = a + fold(low.astype(F32))
             acc[5, :, c : c + 256] += a
         for c in range(0, D, 256):
-            zpart[r, c : c + 256] = dot_nt(dpre[r, :], w_in[c : c + 256, :]).astype(BF16)
-        start_up(4 * i, half - 4 * count, i == count - 1)
-
-        @pl.when(i > 0)
-        def _():
-            zslot(i - 1, total=False)
-
-        return carry
-
-    lax.fori_loop(0, count, forward, 0)
-
-    def partial_out(i, carry):
-        r = pl.ds(pl.multiple_of(i * ROWS, 16), ROWS)
-        ro = pl.ds(pl.multiple_of(R + i * ROWS, 16), ROWS)
+            part = dot_nt(dpre[r, :], w_in[c : c + 256, :])
+            zpart[pl.ds(i * last, last), c : c + 256] = part[0:last].astype(BF16)
+            tails[i, :, c : c + 256] = part[last : last + 8]
+        start_up(chunks_of(d_rows, i))
+
+
+    for i in range(count):
+        forward(i)
+    tick()
+
+    zpart[zrows(seam), :] = pack_tails()
+    start_up([seam])
+
+    def partial_out(i):
+        r = pl.ds(i * ROWS, ROWS)
+        ro = pl.ds(o_rows + i * last, last)
         for c in range(0, D, 256):
-            zpart[ro, c : c + 256] = dot_nn(hid[r, :], w_out[:, c : c + 256]).astype(BF16)
-        start_up(half + 4 * i, half - 4 * count, i == count - 1)
-        return carry
-
-    lax.fori_loop(0, count, partial_out, 0)
-    zslot(2)
-
-    def weight_grad(j, carry):
-        cols = pl.ds(pl.multiple_of(j * 256, 256), 256)
+            part = dot_nn(hid[r, :], w_out[:, c : c + 256])
+            zpart[ro, c : c + 256] = part[0:last].astype(BF16)
+            tails[i, :, c : c + 256] = part[last : last + 8]
+
+    for i in range(count):
+        partial_out(i)
+    tick()
+    zpart[zrows(seam + 1), :] = pack_tails()
+    start_up(range(seam + 1, steps))
+
+    def weight_grad(j):
+        cols = pl.ds(j * 256, 256)
         gw[0, cols, :] = dot_tn(chan[:, cols], dpre[...])
         gw[1, cols, :] = dot_tn(dout[:, cols], hid[...])
-        return carry
-
-    lax.fori_loop(0, D // 256, weight_grad, 0)
+
+    for j in range(D // 256):
+        weight_grad(j)
     for c in range(nc):
         rows = pl.ds(pl.multiple_of((2 * c + 1 - core) * shard, 8), shard)
         for m in range(2):
             wsib_s[c, m] = gw[m, rows, :].astype(BF16)
     w_sib = rcopy(wsib_s, wsib_r, w_sem.at[0, 0], w_sem.at[1, 0], (sib, t))
     w_sib.start()
-    zslot(3)
+    tick()
 
     sqs[...] = jnp.zeros(sqs.shape, F32)
 
-    def square(i, carry):
-        r = pl.ds(pl.multiple_of(i * ROWS, 16), ROWS)
+    def square(i):
+        r = pl.ds(i * ROWS, ROWS)
         g1 = dot_nt(chan[r, :], chan[r, :]) * dot_nt(dpre[r, :], dpre[r, :])
         g2 = dot_nt(dout[r, :], dout[r, :]) * dot_nt(hid[r, :], hid[r, :])
         sqs[pl.ds(i, 1), 0:ROWS] = jnp.sum(g1 + g2, axis=0, keepdims=True)
-        return carry
-
-    lax.fori_loop(0, count, square, 0)
-    zslot(4)
+
+    for i in range(count):
+        square(i)
+    tick()
 
     w_sib.wait_recv()
 
@@ -484,72 +522,71 @@
         return gw[m, rows, :] + wsib_r[dest, m].astype(F32)
 
     first, second = 1 + core, 2 - core
+
+    infl[...] = jnp.zeros(infl.shape, F32)
+
+    def query(j):
+        k = j // 2
+        if j == 0:
+            slot, cin, din, hid_q, pre_q = me, chan, dout, hid, dpre
+        else:
+            slot = peer_sib(k) if j % 2 else peer(k)
+            if j % 2:
+                dqs.from_sib(k)
+                cqs.from_sib(k)
+            cin, din, hid_q, pre_q = cq.at[slot], dq.at[slot], hq, pq
+            for c in range(0, D, 256):
+                tmp[0:ROWS, :] = dot_nn(cin[...], w_in[:, c : c + 256])
+                tmp[ROWS : 2 * ROWS, :] = dot_nt(din[...], w_out[c : c + 256, :])
+                for b in range(0, ROWS, 16):
+                    value, slope = gelu_pair(tmp[b : b + 16, :] + bs[0:1, c : c + 256])
+                    hq[b : b + 16, c : c + 256] = value.astype(BF16)
+                    pq[b : b + 16, c : c + 256] = (slope * tmp[ROWS + b : ROWS + b + 16, :]).astype(BF16)
+        for q in range(count - QRY_DEV):
+            r = slice((QRY_DEV + q) * ROWS, (QRY_DEV + q + 1) * ROWS)
+            g1 = dot_nt(cin[0:ROWS, :], chan[r, :]) * dot_nt(pre_q[0:ROWS, :], dpre[r, :])
+            g2 = dot_nt(din[0:ROWS, :], dout[r, :]) * dot_nt(hid_q[0:ROWS, :], hid[r, :])
+            infl[q, pl.ds(slot, 1), 0:ROWS] = jnp.sum(g1 + g2, axis=0, keepdims=True)
+        tick()
+
+    dqs.relay(1)
+    dqs.relay(2)
+    query(0)
+    query(1)
+    tick()
+    cqs.relay(1)
+    cqs.relay(2)
     for n, dest in ((0, chip ^ 3), (1, chip ^ first)):
         for m in range(2):
             wch_s[n, m] = w_share(dest, m).astype(BF16)
         w_chip(n, first).start()
-
-    infl[...] = jnp.zeros(infl.shape, F32)
-
-    def query(j, carry):
-        k = j // 2
-        own = j % 2 == 0
-        slot = jnp.where(own, peer(k), peer_sib(k))
-
-        @pl.when(jnp.logical_not(own))
-        def _():
-            dqs.from_sib(k)
-            cqs.from_sib(k)
-
-        zslot(j + jnp.where(j < 2, 5, half + LAG + 2))
-        for c in range(0, D, 256):
-            tmp[0:ROWS, :] = dot_nn(cq[slot], w_in[:, c : c + 256])
-            tmp[ROWS : 2 * ROWS, :] = dot_nt(dq[slot], w_out[c : c + 256, :])
-            for b in range(0, ROWS, 16):
-                value, slope = gelu_pair(tmp[b : b + 16, :] + bs[0:1, c : c + 256])
-                hq[b : b + 16, c : c + 256] = value.astype(BF16)
-                pq[b : b + 16, c : c + 256] = (slope * tmp[ROWS + b : ROWS + b + 16, :]).astype(BF16)
-        for q in range(count - QRY_DEV):
-            r = slice((QRY_DEV + q) * ROWS, (QRY_DEV + q + 1) * ROWS)
-            g1 = dot_nt(cq[slot], chan[r, :]) * dot_nt(pq[...], dpre[r, :])
-            g2 = dot_nt(dq[slot], dout[r, :]) * dot_nt(hq[...], hid[r, :])
-            infl[q, pl.ds(slot, 1), 0:ROWS] = jnp.sum(g1 + g2, axis=0, keepdims=True)
-        return carry
-
-    lax.fori_loop(0, 2, query, 0)
-    for s in range(7, half + LAG):
-        zslot(s)
-        if s == 7:
-            for k in (1, 2):
-                dqs.relay(k)
-        if s == 9:
-            dqs.relay(3)
-            for k in (1, 2):
-                cqs.relay(k)
-        if s == 11:
-            w_chip(0, first).wait_recv()
-            for m in range(2):
-                wch_s[2, m] = (w_share(chip ^ second, m) + wch_r[0, m].astype(F32)).astype(BF16)
-            w_chip(2, second).start()
+    for j in (2, 4, 3, 5):
+        query(j)
+    tick(until=seam)
 
     gtok[...] = jnp.zeros(gtok.shape, F32)
 
     def ing_copy(i):
         return pltpu.make_async_copy(ing_s.at[i], ing_o.at[i], out_sem.at[0, i])
 
-    def backward(i, carry):
-        @pl.when(i == 0)
-        def _():
-            zfin(0, 1)
-
-        zfin(4 * i + 1, 4)
-        base = pl.multiple_of(i * ROWS, 16)
+    zfin([seam])
+    rest = ztot[zrows(seam), :].astype(F32)
+    for i in range(count):
+        rests[i, 0:tail, :] = rest[tail * i : tail * (i + 1)]
+        rests[i, tail:16, :] = jnp.zeros((16 - tail, D), F32)
+
+    def backward(i):
+        zfin(chunks_of(d_rows, i))
+        base = i * ROWS
         r = pl.ds(base, ROWS)
         a1 = jnp.zeros((8, D), F32)
         a3 = jnp.zeros((8, D), F32)
         for b in range(nblk):
             rb = pl.ds(base + 16 * b, 16)
-            e = ztot[rb, :].astype(F32)
+            if b < nblk - 1:
+                e = ztot[pl.ds(i * last + 16 * b, 16), :].astype(F32)
+            else:
+                e = rests[i]
             xhat = xh2[rb, :]
             a1 = a1 + fold(e * xhat)
             a3 = a3 + fold(e)
@@ -588,10 +625,18 @@
         acc[0] += a0
         acc[2] += a2
         ing_copy(i).start()
-        zslot(half + LAG + i)
-        return carry
-
-    lax.fori_loop(0, count, backward, 0)
+        tick()
+
+    for i in range(count):
+        backward(i)
+        if i == 0:
+            dqs.relay(3)
+            cqs.relay(3)
+        if i == 1:
+            w_chip(0, first).wait_recv()
+            for m in range(2):
+                wch_s[2, m] = (w_share(chip ^ second, m) + wch_r[0, m].astype(F32)).astype(BF16)
+            w_chip(2, second).start()
 
     for c in range(nc):
         rows = pl.ds(pl.multiple_of((2 * c + 1 - core) * kb, 8), kb)
@@ -605,7 +650,7 @@
     vec[6:7, 0:256] = gtok[1, K : K + 1, :]
     v_sib = rcopy(vec, vsib_r, v_sem.at[0, 0], v_sem.at[1, 0], (sib, t))
     v_sib.start()
-    zslot(half + LAG + count)
+    tick()
     v_sib.wait_recv()
 
     def v_chip(k):
@@ -631,9 +676,25 @@
         t_chip(k).start()
 
 
-    cqs.relay(3)
-    lax.fori_loop(2, n_dp, query, 0)
-    at = half + LAG + 2 + n_dp
+    def act_copy(i):
+        return pltpu.make_async_copy(act_s.at[i], act_o.at[i], out_sem.at[1, i])
+
+    def act(i):
+        tick(chunks_of(o_rows, i)[-1])
+        zfin([seam + 1] * (i == 0) + chunks_of(o_rows, i))
+        start = o_rows + i * last
+        for b in range(0, last, 16):
+            ro = slice(start + b, start + b + 16)
+            a = xf[i * ROWS + b : i * ROWS + b + 16, :] + ztot[ro, :].astype(F32) + bs[1:2, :]
+            act_s[i, b : b + 16, :] = a.astype(BF16)
+        a = ztot[zrows(seam + 1), :].astype(F32)[tail * i : tail * (i + 1)] + bs[1:2, :]
+        a = a + xf[i * ROWS + last : i * ROWS + patches, :]
+        act_s[i, last:patches, :] = a.astype(BF16)
+        act_copy(i).start()
+
+    act(0)
+    query(6)
+    query(7)
 
     def as_row(values):
         totals = jnp.sum(values, axis=1, keepdims=True)
@@ -660,7 +721,7 @@
         w_chip(n, first).wait_recv()
         for m, out in enumerate((gwi_o, gwo_o)):
             out[...] += wch_r[n, m].astype(F32)
-    zslot(at)
+    act(1)
     for k in (1, 2, 3):
         sm_copy(k).wait_recv()
     sm_o[...] = (zsm[0] + zsm[1]) + (zsm[2] + zsm[3])
@@ -680,45 +741,20 @@
     vec_o[...] = pltpu.roll(total, (D - me * shard) % D, 1)[:, 0:128]
 
 
-    def act_copy(i):
-        return pltpu.make_async_copy(act_s.at[i], act_o.at[i], out_sem.at[1, i])
-
-    at += 1
-    for i in range(count):
-        need = -(-((i + 1) * ROWS) // CHUNK) + half
-        while at < min(need + LAG, steps + LAG):
-            zslot(at)
-            at += 1
-        first = half if i == 0 else -(-(i * ROWS) // CHUNK) + half
-        zfin(first, need - first)
-        for b in range(nblk):
-            n = min(16, patches - 16 * b)
-            rb = slice(i * ROWS + 16 * b, i * ROWS + 16 * b + 16)
-            ro = slice(R + i * ROWS + 16 * b, R + i * ROWS + 16 * b + 16)
-            a = (xf[rb, :] + ztot[ro, :].astype(F32) + bs[1:2, :]).astype(BF16)
-            act_s[i, 16 * b : 16 * b + n, :] = a[0:n]
-        act_copy(i).start()
+    act(count - 1)
 
     params.drain()
     dqs.drain()
     cqs.drain()
 
-    def drain_end(c, carry):
-        up_copy(c).wait_send()
-        return carry
-
-    def drain_mid(c, carry):
-        mid_copy(c).wait_send()
-        down_copy(c).wait_send()
-        return carry
-
     @pl.when(end)
     def _():
-        lax.fori_loop(0, steps, drain_end, 0)
+        rcopy(zpart, zrx, z_sent.at[0], z_sem.at[0, 0], (me, end_peer)).wait_send()
 
     @pl.when(mid)
     def _():
-        lax.fori_loop(0, steps, drain_mid, 0)
+        rcopy(zpair, zrxp, z_sent.at[1], z_sem.at[1, 0], (me, mid_peer)).wait_send()
+        rcopy(ztot, ztot, z_sent.at[2], z_sem.at[2, 0], (me, mid_end)).wait_send()
 
     w_sib.wait_send()
     t_sib.wait_send()
@@ -734,20 +770,35 @@
         act_copy(i).wait()
 
 
-def finish(shard, ks, patches, count, queries, act, ing, gwi, gwo, gti, gto, vec, tbo, sm, *refs):
-    big, small, held, sem = refs[:4], refs[4:14], refs[14:18], refs[18]
+def finish(shard, ks, patches, count, queries, act, ing, gwi, gwo, gti_h, gto_h, vec_h, tbo_h, sm_h, *refs):
+    big, small, refs = refs[:4], refs[4:14], refs[14:]
+    held, got, made, sem = refs[:4], refs[4:9], refs[9:19], refs[19]
     pieces = [(n, i) for n in (0, 1) for i in range(count)] + [(2, None), (3, None)]
 
     def part(ref, i):
         return ref if i is None else ref.at[i]
 
-    loads, stores = [], []
-    for at, (n, i) in enumerate(pieces):
-        kept = part(held[n], i)
-        loads.append(pltpu.make_async_copy(part((act, ing, gwi, gwo)[n], i), kept, sem.at[0, at]))
-        stores.append(pltpu.make_async_copy(kept, part(big[n], i), sem.at[1, at]))
-        loads[-1].start()
-    gains, shifts, gti_o, gto_o, gtb_o, tbo_o, gbi_o, gbo_o, sq_o, infl_o = small
+    loads = [
+        pltpu.make_async_copy(a, b, sem.at[0, n])
+        for n, (a, b) in enumerate(zip((gti_h, gto_h, vec_h, tbo_h, sm_h), got))
+    ]
+    moves = []
+    for n, i in pieces:
+        kept, at = part(held[n], i), len(moves)
+        moves.append(
+            (
+                pltpu.make_async_copy(part((act, ing, gwi, gwo)[n], i), kept, sem.at[1, at]),
+                pltpu.make_async_copy(kept, part(big[n], i), sem.at[2, at]),
+            )
+        )
+    for c in loads:
+        c.start()
+    for load, _ in moves:
+        load.start()
+    for c in loads:
+        c.wait()
+    gti, gto, vec, tbo, sm = got
+    gains, shifts, gti_o, gto_o, gtb_o, tbo_o, gbi_o, gbo_o, sq_o, infl_o = made
     gains[...] = vec[0:2, 0:shard]
     shifts[...] = vec[2:4, 0:shard]
     gbo_o[...] = vec[4:5, 0:shard]
@@ -761,11 +812,14 @@
     sq_o[...] = sm[0:1, 0:count]
     for t in range(infl_o.shape[0]):
         infl_o[t : t + 1, :] = sm[1 + t : 2 + t, 0:queries]
-    for load, store in zip(loads, stores):
+    stores = [pltpu.make_async_copy(a, b, sem.at[3, n]) for n, (a, b) in enumerate(zip(made, small))]
+    for c in stores:
+        c.start()
+    for load, store in moves:
         load.wait()
         store.start()
-    for store in stores:
-        store.wait()
+    for c in stores + [store for _, store in moves]:
+        c.wait()
 
 
 def fused(
@@ -792,7 +846,7 @@
     KA = K + 16
     KL = -(-KA // 128) * 128
     R = count * ROWS
-    steps = 2 * (R // CHUNK)
+    zrows, steps = sum(z_sizes(count)), len(z_sizes(count))
     shard = width // n_dp
     hidden = w_in.shape[1]
     anyspace = pl.BlockSpec(memory_space=pl.ANY)
@@ -800,6 +854,14 @@
     V = pltpu.VMEM
     dma = lambda *s: pltpu.SemaphoreType.DMA(s)
     scratch = dict(
+        gains_r=V(norm_gains.shape, BF16),
+        shifts_r=V(norm_shifts.shape, BF16),
+        tok_in_r=V((ks, patches), BF16),
+        tok_out_r=V((ks, patches), BF16),
+        tok_bias_r=V(tok_bias_in.shape, BF16),
+        tok_bias_out_r=V(tok_bias_out.shape, BF16),
+        bias_in_r=V(bias_in.shape, BF16),
+        bias_out_r=V(bias_out.shape, BF16),
         x_raw=V((count, patches, D), BF16),
         d_raw=V((count, patches, D), BF16),
         w_in=V((D, hidden), BF16),
@@ -838,11 +900,13 @@
         dmix=V((ROWS, D), BF16),
         dtok=V((K, D), BF16),
         dnorm=V((ROWS, D), F32),
-        zpart=V((2 * R, D), BF16),
-        zrx=V((2 * R, D), BF16),
-        zpair=V((2 * R, D), BF16),
-        zrxp=V((2 * R, D), BF16),
-        ztot=V((2 * R, D), BF16),
+        tails=V((count, 8, D), F32),
+        rests=V((count, 16, D), F32),
+        zpart=V((zrows, D), BF16),
+        zrx=V((zrows, D), BF16),
+        zpair=V((zrows, D), BF16),
+        zrxp=V((zrows, D), BF16),
+        ztot=V((zrows, D), BF16),
         gw=V((2, D, hidden), F32),
         wsib_s=V((nc, 2, shard, hidden), BF16),
         wsib_r=V((nc, 2, shard, hidden), BF16),
@@ -858,17 +922,13 @@
         vsib_r=V((8, D), F32),
         vch=V((nc, 8, D), F32),
         zsm=V((4, 8, 128), F32),
-        in_sem=dma(4),
+        in_sem=dma(12),
         out_sem=dma(2, count),
-        pb_c=dma(2, nc - 1),
-        pb_x=dma(2, nc),
-        dq_c=dma(2, nc - 1),
-        dq_x=dma(2, nc),
-        cq_c=dma(2, nc - 1),
-        cq_x=dma(2, nc),
-        ze=dma(2, steps),
-        zm=dma(2, steps),
-        zt=dma(2, steps),
+        pb_sem=dma(8),
+        dq_sem=dma(8),
+        cq_sem=dma(8),
+        z_sem=dma(3, steps),
+        z_sent=dma(3),
         w_sem=dma(2, nc),
         t_sem=dma(2, nc),
         v_sem=dma(2, nc),
@@ -894,7 +954,7 @@
     act, ing, gwi, gwo, gti, gto, vec, tbo, sm = pl.pallas_call(
         body,
         out_shape=[jax.ShapeDtypeStruct(s, d) for s, d, _ in outs],
-        in_specs=[anyspace] * 4 + [vm] * 8,
+        in_specs=[anyspace] * 12,
         out_specs=[o[2] for o in outs],
         scratch_shapes=list(scratch.values()),
         compiler_params=pltpu.CompilerParams(
@@ -916,36 +976,29 @@
         bias_out,
     )
     queries, trains = n_dp * QRY_DEV, count - QRY_DEV
+    shapes = [
+        (images.shape, BF16),
+        (images.shape, BF16),
+        ((shard, hidden), F32),
+        ((shard, hidden), F32),
+        ((2, shard), F32),
+        ((2, shard), F32),
+        ((ks, patches), F32),
+        ((ks, patches), F32),
+        ((1, ks), F32),
+        ((1, patches), F32),
+        ((1, shard), F32),
+        ((1, shard), F32),
+        ((1, count), F32),
+        ((trains, queries), F32),
+    ]
+    smalls = [(o.shape, F32) for o in (gti, gto, vec, tbo, sm)]
     out = pl.pallas_call(
         functools.partial(finish, shard, ks, patches, count, queries),
-        out_shape=[
-            jax.ShapeDtypeStruct(s, d)
-            for s, d in (
-                (images.shape, BF16),
-                (images.shape, BF16),
-                ((shard, hidden), F32),
-                ((shard, hidden), F32),
-                ((2, shard), F32),
-                ((2, shard), F32),
-                ((ks, patches), F32),
-                ((ks, patches), F32),
-                ((1, ks), F32),
-                ((1, patches), F32),
-                ((1, shard), F32),
-                ((1, shard), F32),
-                ((1, count), F32),
-                ((trains, queries), F32),
-            )
-        ],
-        in_specs=[anyspace] * 4 + [vm] * 5,
-        out_specs=[anyspace] * 4 + [vm] * 10,
-        scratch_shapes=[
-            V(images.shape, BF16),
-            V(images.shape, BF16),
-            V((shard, hidden), F32),
-            V((shard, hidden), F32),
-            dma(2, 2 * count + 2),
-        ],
+        out_shape=[jax.ShapeDtypeStruct(s, d) for s, d in shapes],
+        in_specs=[anyspace] * 9,
+        out_specs=[anyspace] * 14,
+        scratch_shapes=[V(s, d) for s, d in shapes[:4] + smalls + shapes[4:]] + [dma(4, 10)],
         name="finish",
     )(act, ing, gwi, gwo, gti, gto, vec, tbo, sm)
     act, ing, gwi, gwo, gains, shifts, gti, gto, gtb, tbo, gbi, gbo, squares, influence = out

time: 81.9 us -> 72.8 us (0.89)
  Pallas kernels: 81 us -> 71.8 us
    pallas_call x1, Pallas kernels: 76.9 us -> 69 us  [fused(): pl.pallas_call(body, out_shape=[jax.ShapeDtypeStruct(s, d) for s, d, _ in...]
    pallas_call x1, Pallas kernels: 4.05 us -> 2.83 us  [fused(): pl.pallas_call(functools.partial(finish, shard, ks, patches, count, queri...]
where the time goes in v3:
time: 72.8 us; the launch traced here: 72.6 us
  Pallas kernels  71.8 us (99%)
  between operations  0.84 us (1%)
    pallas_call x1, Pallas kernels, fused(): pl.pallas_call(body, out_shape=[jax.ShapeDtypeStruct(s, d) for s, d, _ in...  69 us
    pallas_call x1, Pallas kernels, fused(): pl.pallas_call(functools.partial(finish, shard, ks, patches, count, queri...  2.83 us

profile of v3, /device:TPU:0, one launch (start us, length us, event | category | flops | bytes accessed | tf_op | source)
XLA Modules:
  0.0 72.6 jit_solution(9600079095051012064)
XLA Ops:
  0.6 69.0 %mixer.1 = (bf16[3,196,768]{2,1,0:T(8,128)(2,1)}, bf16[3,196,768]{2,1,0:T(8,128)(2,1)}, f32[96,768]{1,0:T(8,128)}, f32[96,768]{1,0:T(8,128)}, f32[48,256]{1,0:T(...) custom-call(bf16[3,196,768]{2,1,0:T(8,128)(2,1)} %refs_0_.1, ...), custom_call_target="tpu_custom_call" | custom-call | tf_op jit(solution)/shard_map/mixer/pallas_call | solution.py:954
  69.6 2.8 %finish.1 = (bf16[3,196,768]{2,1,0:T(8,128)(2,1)}, bf16[3,196,768]{2,1,0:T(8,128)(2,1)}, f32[96,768]{1,0:T(8,128)}, f32[96,768]{1,0:T(8,128)}, f32[2,96]{1,0:T(2...) custom-call(bf16[3,196,768]{2,1,0:T(8,128)(2,1)} %get-tuple-element., ...), custom_call_target="tpu_custom_call" | custom-call | tf_op jit(solution)/shard_map/finish/pallas_call | solution.py:996

commit v4 on v3

--- a/solution.py
+++ b/solution.py
@@ -79,6 +79,13 @@
     vec_o,
     tbo_o,
     sm_o,
+    gwi_k,
+    gwo_k,
+    gti_k,
+    gto_k,
+    vec_k,
+    tbo_k,
+    sm_k,
     gains_r,
     shifts_r,
     tok_in_r,
@@ -149,6 +156,7 @@
     zsm,
     in_sem,
     out_sem,
+    small_sem,
     pb_sem,
     dq_sem,
     cq_sem,
@@ -387,11 +395,15 @@
 
     slots = [[c] for c in range(seam)] + [[seam, seam + 1]] + [[c] for c in range(seam + 2, steps)]
     ticks = iter(range(len(slots) + 2))
+    totals = set()
 
     def tick(until=None):
+        if until in totals:
+            return
         for n in ticks:
             ups = slots[n] if n < len(slots) else []
             downs = slots[n - 2] if n >= 2 else []
+            totals.update(downs)
 
             @pl.when(mid)
             def _():
@@ -547,12 +559,13 @@
             g1 = dot_nt(cin[0:ROWS, :], chan[r, :]) * dot_nt(pre_q[0:ROWS, :], dpre[r, :])
             g2 = dot_nt(din[0:ROWS, :], dout[r, :]) * dot_nt(hid_q[0:ROWS, :], hid[r, :])
             infl[q, pl.ds(slot, 1), 0:ROWS] = jnp.sum(g1 + g2, axis=0, keepdims=True)
-        tick()
 
     dqs.relay(1)
     dqs.relay(2)
     query(0)
+    tick()
     query(1)
+    tick()
     tick()
     cqs.relay(1)
     cqs.relay(2)
@@ -562,6 +575,7 @@
         w_chip(n, first).start()
     for j in (2, 4, 3, 5):
         query(j)
+        tick()
     tick(until=seam)
 
     gtok[...] = jnp.zeros(gtok.shape, F32)
@@ -650,6 +664,7 @@
     vec[6:7, 0:256] = gtok[1, K : K + 1, :]
     v_sib = rcopy(vec, vsib_r, v_sem.at[0, 0], v_sem.at[1, 0], (sib, t))
     v_sib.start()
+    query(6)
     tick()
     v_sib.wait_recv()
 
@@ -674,7 +689,35 @@
         for m in range(2):
             tch_s[k - 1, m] = gtok[m, rows, :] + tsib_r[dest, m]
         t_chip(k).start()
-
+    query(7)
+
+    def as_row(values):
+        totals = jnp.sum(values, axis=1, keepdims=True)
+        at = lax.broadcasted_iota(jnp.int32, (values.shape[0], 128), 0)
+        lane = lax.broadcasted_iota(jnp.int32, (values.shape[0], 128), 1)
+        return jnp.sum(jnp.where(at == lane, totals, 0.0), axis=0, keepdims=True)
+
+    zsm[t] = jnp.zeros((8, 128), F32)
+    zsm[t, 0:1, :] = as_row(sqs[...]) / (2.0 * D * FF)
+    for q in range(count - QRY_DEV):
+        zsm[t, 1 + q : 2 + q, :] = as_row(infl[q]) * (2.0 * D * FF) ** (-0.5)
+
+    def sm_copy(k):
+        return rcopy(
+            zsm.at[t], zsm.at[t], s_sem.at[0, k - 1], s_sem.at[1, k - 1], (me, (t + k) % 4)
+        )
+
+    for k in (1, 2, 3):
+        sm_copy(k).start()
+
+    tick()
+
+    for m, out in enumerate((gwi_k, gwo_k)):
+        out[...] = w_share(chip, m)
+    for n in (1, 2):
+        w_chip(n, first).wait_recv()
+        for m, out in enumerate((gwi_k, gwo_k)):
+            out[...] += wch_r[n, m].astype(F32)
 
     def act_copy(i):
         return pltpu.make_async_copy(act_s.at[i], act_o.at[i], out_sem.at[1, i])
@@ -693,54 +736,30 @@
         act_copy(i).start()
 
     act(0)
-    query(6)
-    query(7)
-
-    def as_row(values):
-        totals = jnp.sum(values, axis=1, keepdims=True)
-        at = lax.broadcasted_iota(jnp.int32, (values.shape[0], 128), 0)
-        lane = lax.broadcasted_iota(jnp.int32, (values.shape[0], 128), 1)
-        return jnp.sum(jnp.where(at == lane, totals, 0.0), axis=0, keepdims=True)
-
-    zsm[t] = jnp.zeros((8, 128), F32)
-    zsm[t, 0:1, :] = as_row(sqs[...]) / (2.0 * D * FF)
-    for q in range(count - QRY_DEV):
-        zsm[t, 1 + q : 2 + q, :] = as_row(infl[q]) * (2.0 * D * FF) ** (-0.5)
-
-    def sm_copy(k):
-        return rcopy(
-            zsm.at[t], zsm.at[t], s_sem.at[0, k - 1], s_sem.at[1, k - 1], (me, (t + k) % 4)
-        )
-
-    for k in (1, 2, 3):
-        sm_copy(k).start()
-
-    for m, out in enumerate((gwi_o, gwo_o)):
-        out[...] = w_share(chip, m)
-    for n in (1, 2):
-        w_chip(n, first).wait_recv()
-        for m, out in enumerate((gwi_o, gwo_o)):
-            out[...] += wch_r[n, m].astype(F32)
+    tick()
     act(1)
+
     for k in (1, 2, 3):
         sm_copy(k).wait_recv()
-    sm_o[...] = (zsm[0] + zsm[1]) + (zsm[2] + zsm[3])
+    sm_k[...] = (zsm[0] + zsm[1]) + (zsm[2] + zsm[3])
     rows = pl.ds(pl.multiple_of(me * kb, 8), kb)
-    for m, out in enumerate((gti_o, gto_o)):
+    for m, out in enumerate((gti_k, gto_k)):
         out[...] = gtok[m, rows, :] + tsib_r[chip, m]
     for k in range(1, nc):
         t_chip(k).wait_recv()
-        for m, out in enumerate((gti_o, gto_o)):
+        for m, out in enumerate((gti_k, gto_k)):
             out[...] += tch_r[k - 1, m]
     for k in range(1, nc):
         v_chip(k).wait_recv()
     total = vch[0]
     for c in range(1, nc):
         total = total + vch[c]
-    tbo_o[...] = total[:, 0:256]
-    vec_o[...] = pltpu.roll(total, (D - me * shard) % D, 1)[:, 0:128]
-
-
+    tbo_k[...] = total[:, 0:256]
+    vec_k[...] = pltpu.roll(total, (D - me * shard) % D, 1)[:, 0:128]
+    stores = [(gwi_k, gwi_o), (gwo_k, gwo_o), (gti_k, gti_o), (gto_k, gto_o), (vec_k, vec_o), (tbo_k, tbo_o), (sm_k, sm_o)]
+    stores = [pltpu.make_async_copy(a, b, small_sem.at[n]) for n, (a, b) in enumerate(stores)]
+    for c in stores:
+        c.start()
     act(count - 1)
 
     params.drain()
@@ -765,6 +784,8 @@
         v_chip(k).wait_send()
     for k in (1, 2, 3):
         sm_copy(k).wait_send()
+    for c in stores:
+        c.wait()
     for i in range(count):
         ing_copy(i).wait()
         act_copy(i).wait()
@@ -850,10 +871,16 @@
     shard = width // n_dp
     hidden = w_in.shape[1]
     anyspace = pl.BlockSpec(memory_space=pl.ANY)
-    vm = pl.BlockSpec(memory_space=pltpu.VMEM)
     V = pltpu.VMEM
     dma = lambda *s: pltpu.SemaphoreType.DMA(s)
     scratch = dict(
+        gwi_k=V((shard, hidden), F32),
+        gwo_k=V((shard, hidden), F32),
+        gti_k=V((kb, 256), F32),
+        gto_k=V((kb, 256), F32),
+        vec_k=V((8, 128), F32),
+        tbo_k=V((8, 256), F32),
+        sm_k=V((8, 128), F32),
         gains_r=V(norm_gains.shape, BF16),
         shifts_r=V(norm_shifts.shape, BF16),
         tok_in_r=V((ks, patches), BF16),
@@ -924,6 +951,7 @@
         zsm=V((4, 8, 128), F32),
         in_sem=dma(12),
         out_sem=dma(2, count),
+        small_sem=dma(7),
         pb_sem=dma(8),
         dq_sem=dma(8),
         cq_sem=dma(8),
@@ -937,13 +965,13 @@
     outs = [
         (images.shape, BF16, anyspace),
         (images.shape, BF16, anyspace),
-        ((shard, hidden), F32, vm),
-        ((shard, hidden), F32, vm),
-        ((kb, 256), F32, vm),
-        ((kb, 256), F32, vm),
-        ((8, 128), F32, vm),
-        ((8, 256), F32, vm),
-        ((8, 128), F32, vm),
+        ((shard, hidden), F32, anyspace),
+        ((shard, hidden), F32, anyspace),
+        ((kb, 256), F32, anyspace),
+        ((kb, 256), F32, anyspace),
+        ((8, 128), F32, anyspace),
+        ((8, 256), F32, anyspace),
+        ((8, 128), F32, anyspace),
     ]
     names = list(scratch)
     n_in, n_out = 12, len(outs)

time: 72.8 us -> 70 us (0.962)
  Pallas kernels: 71.8 us -> 69 us
    pallas_call x1, Pallas kernels: 69 us -> 66.2 us  [fused(): pl.pallas_call(body, out_shape=[jax.ShapeDtypeStruct(s, d) for s, d, _ in...]
where the time goes in v4:
time: 70 us; the launch traced here: 69.8 us
  Pallas kernels  69 us (99%)
  between operations  0.84 us (1%)
    pallas_call x1, Pallas kernels, fused(): pl.pallas_call(body, out_shape=[jax.ShapeDtypeStruct(s, d) for s, d, _ in...  66.2 us
    pallas_call x1, Pallas kernels, fused(): pl.pallas_call(functools.partial(finish, shard, ks, patches, count, queri...  2.83 us

profile of v4, /device:TPU:0, one launch (start us, length us, event | category | flops | bytes accessed | tf_op | source)
XLA Modules:
  0.0 69.8 jit_solution(8006739443155578481)
XLA Ops:
  0.6 66.2 %mixer.1 = (bf16[3,196,768]{2,1,0:T(8,128)(2,1)}, bf16[3,196,768]{2,1,0:T(8,128)(2,1)}, f32[96,768]{1,0:T(8,128)}, f32[96,768]{1,0:T(8,128)}, f32[48,256]{1,0:T(...) custom-call(bf16[3,196,768]{2,1,0:T(8,128)(2,1)} %refs_0_.1, ...), custom_call_target="tpu_custom_call" | custom-call | tf_op jit(solution)/shard_map/mixer/pallas_call | solution.py:982
  66.8 2.8 %finish.1 = (bf16[3,196,768]{2,1,0:T(8,128)(2,1)}, bf16[3,196,768]{2,1,0:T(8,128)(2,1)}, f32[96,768]{1,0:T(8,128)}, f32[96,768]{1,0:T(8,128)}, f32[2,96]{1,0:T(2...) custom-call(bf16[3,196,768]{2,1,0:T(8,128)(2,1)} %get-tuple-element., ...), custom_call_target="tpu_custom_call" | custom-call | tf_op jit(solution)/shard_map/finish/pallas_call | solution.py:1024

commit v5 on v4

--- a/solution.py
+++ b/solution.py
@@ -348,7 +348,6 @@
     ri = lax.broadcasted_iota(jnp.int32, (ROWS, ROWS), 0)
     ci = lax.broadcasted_iota(jnp.int32, (ROWS, ROWS), 1)
     eye_rows = ((ri == ci) & (ri < patches)).astype(BF16)
-    toki[:, 0:K] = dot_nt(eye_rows, toki_t[:, 0:ROWS]).astype(BF16)
     toko[:, 0:KA] = dot_nt(eye_rows, toko_t[:, 0:ROWS]).astype(BF16)
 
     chunks = []
@@ -373,7 +372,7 @@
         return rcopy(zpair.at[r], zrxp.at[r], z_sent.at[1], z_sem.at[1, c], (me, mid_peer))
 
     def down_copy(c, r):
-        return rcopy(ztot.at[r], ztot.at[r], z_sent.at[2], z_sem.at[2, c], (me, mid_end))
+        return rcopy(ztot.at[r], ztot.at[r], z_sent.at[0], z_sem.at[0, c], (me, mid_end))
 
     def start_up(some):
         @pl.when(end)
@@ -579,6 +578,7 @@
     tick(until=seam)
 
     gtok[...] = jnp.zeros(gtok.shape, F32)
+    toki[:, 0:K] = dot_nt(eye_rows, toki_t[:, 0:ROWS]).astype(BF16)
 
     def ing_copy(i):
         return pltpu.make_async_copy(ing_s.at[i], ing_o.at[i], out_sem.at[0, i])
@@ -722,22 +722,30 @@
     def act_copy(i):
         return pltpu.make_async_copy(act_s.at[i], act_o.at[i], out_sem.at[1, i])
 
-    def act(i):
-        tick(chunks_of(o_rows, i)[-1])
-        zfin([seam + 1] * (i == 0) + chunks_of(o_rows, i))
-        start = o_rows + i * last
-        for b in range(0, last, 16):
-            ro = slice(start + b, start + b + 16)
+    def act_rows(i, lo, hi):
+        for b in range(lo, hi, 16):
+            ro = slice(o_rows + i * last + b, o_rows + i * last + b + 16)
             a = xf[i * ROWS + b : i * ROWS + b + 16, :] + ztot[ro, :].astype(F32) + bs[1:2, :]
             act_s[i, b : b + 16, :] = a.astype(BF16)
+
+    def act(i):
+        *before, final = chunks_of(o_rows, i)
+        cut = chunks[final][0] - o_rows - i * last
+        tick(before[-1])
+        zfin([seam + 1] * (i == 0) + before)
+        act_rows(i, 0, cut)
         a = ztot[zrows(seam + 1), :].astype(F32)[tail * i : tail * (i + 1)] + bs[1:2, :]
         a = a + xf[i * ROWS + last : i * ROWS + patches, :]
         act_s[i, last:patches, :] = a.astype(BF16)
+        tick(final)
+        zfin([final])
+        act_rows(i, cut, last)
         act_copy(i).start()
 
     act(0)
     tick()
     act(1)
+    tick()
 
     for k in (1, 2, 3):
         sm_copy(k).wait_recv()
@@ -773,7 +781,7 @@
     @pl.when(mid)
     def _():
         rcopy(zpair, zrxp, z_sent.at[1], z_sem.at[1, 0], (me, mid_peer)).wait_send()
-        rcopy(ztot, ztot, z_sent.at[2], z_sem.at[2, 0], (me, mid_end)).wait_send()
+        rcopy(ztot, ztot, z_sent.at[0], z_sem.at[0, 0], (me, mid_end)).wait_send()
 
     w_sib.wait_send()
     t_sib.wait_send()
@@ -955,8 +963,8 @@
         pb_sem=dma(8),
         dq_sem=dma(8),
         cq_sem=dma(8),
-        z_sem=dma(3, steps),
-        z_sent=dma(3),
+        z_sem=dma(2, steps),
+        z_sent=dma(2),
         w_sem=dma(2, nc),
         t_sem=dma(2, nc),
         v_sem=dma(2, nc),

time: 70 us -> 69.6 us (level)
  no operation moved by 1% of the time
where the time goes in v5:
time: 69.6 us; the launch traced here: 69.4 us
  Pallas kernels  68.6 us (99%)
  between operations  0.84 us (1%)
    pallas_call x1, Pallas kernels, fused(): pl.pallas_call(body, out_shape=[jax.ShapeDtypeStruct(s, d) for s, d, _ in...  65.8 us
    pallas_call x1, Pallas kernels, fused(): pl.pallas_call(functools.partial(finish, shard, ks, patches, count, queri...  2.83 us

profile of v5, /device:TPU:0, one launch (start us, length us, event | category | flops | bytes accessed | tf_op | source)
XLA Modules:
  0.0 69.4 jit_solution(7931452223407020841)
XLA Ops:
  0.6 65.8 %mixer.1 = (bf16[3,196,768]{2,1,0:T(8,128)(2,1)}, bf16[3,196,768]{2,1,0:T(8,128)(2,1)}, f32[96,768]{1,0:T(8,128)}, f32[96,768]{1,0:T(8,128)}, f32[48,256]{1,0:T(...) custom-call(bf16[3,196,768]{2,1,0:T(8,128)(2,1)} %refs_0_.1, ...), custom_call_target="tpu_custom_call" | custom-call | tf_op jit(solution)/shard_map/mixer/pallas_call | solution.py:990
  66.4 2.8 %finish.1 = (bf16[3,196,768]{2,1,0:T(8,128)(2,1)}, bf16[3,196,768]{2,1,0:T(8,128)(2,1)}, f32[96,768]{1,0:T(8,128)}, f32[96,768]{1,0:T(8,128)}, f32[2,96]{1,0:T(2...) custom-call(bf16[3,196,768]{2,1,0:T(8,128)(2,1)} %get-tuple-element., ...), custom_call_target="tpu_custom_call" | custom-call | tf_op jit(solution)/shard_map/finish/pallas_call | solution.py:1032

commit v6 on v5

--- a/solution.py
+++ b/solution.py
@@ -581,7 +581,7 @@
     toki[:, 0:K] = dot_nt(eye_rows, toki_t[:, 0:ROWS]).astype(BF16)
 
     def ing_copy(i):
-        return pltpu.make_async_copy(ing_s.at[i], ing_o.at[i], out_sem.at[0, i])
+        return pltpu.make_async_copy(ing_s.at[i], ing_o.at[i], out_sem.at[0])
 
     zfin([seam])
     rest = ztot[zrows(seam), :].astype(F32)
@@ -704,7 +704,7 @@
 
     def sm_copy(k):
         return rcopy(
-            zsm.at[t], zsm.at[t], s_sem.at[0, k - 1], s_sem.at[1, k - 1], (me, (t + k) % 4)
+            zsm.at[t], zsm.at[t], s_sem.at[0], s_sem.at[k], (me, (t + k) % 4)
         )
 
     for k in (1, 2, 3):
@@ -720,7 +720,7 @@
             out[...] += wch_r[n, m].astype(F32)
 
     def act_copy(i):
-        return pltpu.make_async_copy(act_s.at[i], act_o.at[i], out_sem.at[1, i])
+        return pltpu.make_async_copy(act_s.at[i], act_o.at[i], out_sem.at[1])
 
     def act_rows(i, lo, hi):
         for b in range(lo, hi, 16):
@@ -790,25 +790,25 @@
         w_chip(k - 1, first).wait_send()
         t_chip(k).wait_send()
         v_chip(k).wait_send()
-    for k in (1, 2, 3):
-        sm_copy(k).wait_send()
+    z3 = zsm.at[pl.ds(0, 3)]
+    rcopy(z3, z3, s_sem.at[0], s_sem.at[1], (me, (t + 1) % 4)).wait_send()
     for c in stores:
         c.wait()
-    for i in range(count):
-        ing_copy(i).wait()
-        act_copy(i).wait()
+    pltpu.make_async_copy(ing_s, ing_o, out_sem.at[0]).wait()
+    pltpu.make_async_copy(act_s, act_o, out_sem.at[1]).wait()
 
 
 def finish(shard, ks, patches, count, queries, act, ing, gwi, gwo, gti_h, gto_h, vec_h, tbo_h, sm_h, *refs):
     big, small, refs = refs[:4], refs[4:14], refs[14:]
-    held, got, made, sem = refs[:4], refs[4:9], refs[9:19], refs[19]
+    held, got, made = refs[:4], refs[4:9], refs[9:19]
+    got_sem, load_sem, store_sem, made_sem = refs[19:23]
     pieces = [(n, i) for n in (0, 1) for i in range(count)] + [(2, None), (3, None)]
 
     def part(ref, i):
         return ref if i is None else ref.at[i]
 
     loads = [
-        pltpu.make_async_copy(a, b, sem.at[0, n])
+        pltpu.make_async_copy(a, b, got_sem.at[n])
         for n, (a, b) in enumerate(zip((gti_h, gto_h, vec_h, tbo_h, sm_h), got))
     ]
     moves = []
@@ -816,8 +816,8 @@
         kept, at = part(held[n], i), len(moves)
         moves.append(
             (
-                pltpu.make_async_copy(part((act, ing, gwi, gwo)[n], i), kept, sem.at[1, at]),
-                pltpu.make_async_copy(kept, part(big[n], i), sem.at[2, at]),
+                pltpu.make_async_copy(part((act, ing, gwi, gwo)[n], i), kept, load_sem.at[at]),
+                pltpu.make_async_copy(kept, part(big[n], i), store_sem.at[n]),
             )
         )
     for c in loads:
@@ -841,14 +841,16 @@
     sq_o[...] = sm[0:1, 0:count]
     for t in range(infl_o.shape[0]):
         infl_o[t : t + 1, :] = sm[1 + t : 2 + t, 0:queries]
-    stores = [pltpu.make_async_copy(a, b, sem.at[3, n]) for n, (a, b) in enumerate(zip(made, small))]
+    stores = [pltpu.make_async_copy(a, b, made_sem.at[n]) for n, (a, b) in enumerate(zip(made, small))]
     for c in stores:
         c.start()
     for load, store in moves:
         load.wait()
         store.start()
-    for c in stores + [store for _, store in moves]:
+    for c in stores:
         c.wait()
+    for n in range(4):
+        pltpu.make_async_copy(held[n], big[n], store_sem.at[n]).wait()
 
 
 def fused(
@@ -958,7 +960,7 @@
         vch=V((nc, 8, D), F32),
         zsm=V((4, 8, 128), F32),
         in_sem=dma(12),
-        out_sem=dma(2, count),
+        out_sem=dma(2),
         small_sem=dma(7),
         pb_sem=dma(8),
         dq_sem=dma(8),
@@ -968,7 +970,7 @@
         w_sem=dma(2, nc),
         t_sem=dma(2, nc),
         v_sem=dma(2, nc),
-        s_sem=dma(2, 3),
+        s_sem=dma(4),
     )
     outs = [
         (images.shape, BF16, anyspace),
@@ -1034,7 +1036,7 @@
         out_shape=[jax.ShapeDtypeStruct(s, d) for s, d in shapes],
         in_specs=[anyspace] * 9,
         out_specs=[anyspace] * 14,
-        scratch_shapes=[V(s, d) for s, d in shapes[:4] + smalls + shapes[4:]] + [dma(4, 10)],
+        scratch_shapes=[V(s, d) for s, d in shapes[:4] + smalls + shapes[4:]] + [dma(5), dma(2 * count + 2), dma(4), dma(10)],
         name="finish",
     )(act, ing, gwi, gwo, gti, gto, vec, tbo, sm)
     act, ing, gwi, gwo, gains, shifts, gti, gto, gtb, tbo, gbi, gbo, squares, influence = out

time: 69.6 us -> 69.8 us (level)
  no operation moved by 1% of the time
where the time goes in v6:
time: 69.8 us; the launch traced here: 69.7 us
  Pallas kernels  68.8 us (99%)
  between operations  0.84 us (1%)
    pallas_call x1, Pallas kernels, fused(): pl.pallas_call(body, out_shape=[jax.ShapeDtypeStruct(s, d) for s, d, _ in...  65.7 us
    pallas_call x1, Pallas kernels, fused(): pl.pallas_call(functools.partial(finish, shard, ks, patches, count, queri...  3.14 us

profile of v6, /device:TPU:0, one launch (start us, length us, event | category | flops | bytes accessed | tf_op | source)
XLA Modules:
  0.0 69.7 jit_solution(11678146148013354958)
XLA Ops:
  0.6 65.7 %mixer.1 = (bf16[3,196,768]{2,1,0:T(8,128)(2,1)}, bf16[3,196,768]{2,1,0:T(8,128)(2,1)}, f32[96,768]{1,0:T(8,128)}, f32[96,768]{1,0:T(8,128)}, f32[48,256]{1,0:T(...) custom-call(bf16[3,196,768]{2,1,0:T(8,128)(2,1)} %refs_0_.1, ...), custom_call_target="tpu_custom_call" | custom-call | tf_op jit(solution)/shard_map/mixer/pallas_call | solution.py:992
  66.4 3.1 %finish.1 = (bf16[3,196,768]{2,1,0:T(8,128)(2,1)}, bf16[3,196,768]{2,1,0:T(8,128)(2,1)}, f32[96,768]{1,0:T(8,128)}, f32[96,768]{1,0:T(8,128)}, f32[2,96]{1,0:T(2...) custom-call(bf16[3,196,768]{2,1,0:T(8,128)(2,1)} %get-tuple-element., ...), custom_call_target="tpu_custom_call" | custom-call | tf_op jit(solution)/shard_map/finish/pallas_call | solution.py:1034
